TPU v7x, 32 devices: a whole 2x2x4 slice. The times are simulated.
32 devices in a mesh: mem: 4 (over y, x), col: 8 (over z, core).
Axes of the slice: x: 2, y: 2, z: 4, core: 2. Of those that a mesh axis runs over, the one named last changes fastest.
Arguments:
- prior: float32 [80, 32, 24576], P('mem', 'col'), may hold values from -6 to 6
- obs_column: int32 [2, 512], replicated, may hold values from 0 to 24575, as said below
- obs_level: int32 [2, 512], replicated, may hold values from 0 to 31
- obs_value: float32 [2, 512], replicated, may hold values from -8 to 8
- obs_variance: float32 [2, 512], replicated, may hold values from 0.3 to 3
Outputs:
- analysis: float32 [80, 32, 24576], P('mem', 'col')
Inputs may be any that keep to these rules, and one draw needn't show every extreme that they name: `obs_column`: each batch (row) is sorted in non-decreasing order; the first observation of every batch lies at column 0 and the last at column 24575; several observations may share a column.
All inputs are finite; a program needn't handle non-finite values.
Results may differ from a plain program's by a relative error of at most 0.0001.
Values sent between devices are 32-bit elements; how exact they have to be, the bound alone decides.
A program may use at most 192 MiB of HBM per device.

v0:
```python
from functools import partial

import jax
import jax.numpy as jnp
from jax import lax
from jax.sharding import PartitionSpec as P

NLON = 768
P_SIZE = 512
NB = 2
LOCR = 6


def gc_taper(squared_gap, radius):
    scaled = jnp.sqrt(squared_gap.astype(jnp.float32)) / radius
    near_part = (
        ((-0.25 * scaled + 0.5) * scaled + 0.625) * scaled - 5.0 / 3.0
    ) * scaled * scaled + 1.0
    bounded = jnp.maximum(scaled, 1.0)
    far_part = (
        ((((scaled / 12.0 - 0.5) * scaled + 0.625) * scaled + 5.0 / 3.0) * scaled - 5.0) * scaled
        + 4.0
        - 2.0 / (3.0 * bounded)
    )
    zero_part = jnp.zeros_like(scaled)
    result = jnp.where(
        squared_gap < radius * radius,
        near_part,
        jnp.where(squared_gap < 4 * radius * radius, far_part, zero_part),
    )
    return result


def localize(obs_cols, first_col, count):
    col_index = first_col + jnp.arange(count, dtype=jnp.int32)
    row_gap = col_index[None, :] // NLON - obs_cols[:, None] // NLON
    lon_gap = jnp.abs(col_index[None, :] % NLON - obs_cols[:, None] % NLON)
    lon_gap = jnp.minimum(lon_gap, NLON - lon_gap)
    return gc_taper(row_gap * row_gap + lon_gap * lon_gap, LOCR)


def obs_weights(picked, values, variances, members):
    obs_mean = jnp.mean(picked, axis=0)
    obs_anom = picked - obs_mean[None, :]
    obs_total = jnp.sum(obs_anom * obs_anom, axis=0) / (members - 1) + variances
    mean_gain = (values - obs_mean) / obs_total
    root_gain = 1.0 / (obs_total * (1.0 + jnp.sqrt(variances / obs_total)))
    weights = mean_gain[None, :] - root_gain[None, :] * obs_anom
    return (obs_anom, weights)


def pair_blocks(field, tile_count, column_width):
    own_members, own_levels = (field.shape[0], field.shape[1])
    halves = tile_count // 2
    folded = field.reshape(own_members, own_levels, halves, 2, column_width).transpose(
        0, 1, 3, 2, 4
    )
    return folded.reshape(own_members, own_levels, tile_count, column_width)


def unpair_blocks(field, tile_count, column_width):
    own_members, own_levels = (field.shape[0], field.shape[1])
    halves = tile_count // 2
    folded = field.reshape(own_members, own_levels, 2, halves, column_width).transpose(
        0, 1, 3, 2, 4
    )
    return folded.reshape(own_members, own_levels, tile_count * column_width)


def to_tiles(prior):
    own_members, own_levels, all_columns = prior.shape
    mem_count = lax.axis_size("mem")
    col_count = lax.axis_size("col")
    tile_count = mem_count * col_count
    column_width = all_columns // tile_count
    outgoing = pair_blocks(prior, tile_count, column_width)
    arrived = lax.all_to_all(outgoing, ("mem", "col"), split_axis=2, concat_axis=2, tiled=True)
    arrived = arrived.reshape(own_members, own_levels, mem_count, col_count, column_width)
    arrived = arrived.transpose(2, 0, 3, 1, 4)
    return arrived.reshape(mem_count * own_members, col_count * own_levels, column_width)


def to_owners(field_state):
    members, levels, column_width = field_state.shape
    mem_count = lax.axis_size("mem")
    col_count = lax.axis_size("col")
    tile_count = mem_count * col_count
    own_members = members // mem_count
    own_levels = levels // col_count
    outgoing = field_state.reshape(mem_count, own_members, col_count, own_levels, column_width)
    outgoing = outgoing.transpose(1, 3, 0, 2, 4).reshape(
        own_members, own_levels, tile_count, column_width
    )
    arrived = lax.all_to_all(outgoing, ("mem", "col"), split_axis=2, concat_axis=2, tiled=True)
    return unpair_blocks(arrived, tile_count, column_width)


def apply_block(current, anom_part, weight_part, col_part, anomalies, first_col):
    members = current.shape[0]
    column_width = current.shape[2]
    covariance = jnp.einsum(
        "kp,klc->plc",
        anom_part,
        anomalies,
        precision=lax.Precision.HIGHEST,
        preferred_element_type=jnp.float32,
    ) / (members - 1)
    gain_block = covariance * localize(col_part, first_col, column_width)[:, None, :]
    return current + jnp.einsum(
        "kp,plc->klc",
        weight_part,
        gain_block,
        precision=lax.Precision.HIGHEST,
        preferred_element_type=jnp.float32,
    )


def local(prior, obs_column, obs_level, obs_value, obs_variance):
    field_state = to_tiles(prior)
    members, levels, column_width = field_state.shape
    tile_index = lax.axis_index(("mem", "col"))
    halves = lax.axis_size("mem") * lax.axis_size("col") // 2
    block_index = 2 * (tile_index % halves) + tile_index // halves
    first_col = block_index * column_width
    obs_step = min(P_SIZE, 128)
    for batch_index in range(NB):
        flattened = field_state.reshape(members, levels * column_width)
        columns = obs_column[batch_index]
        local_col = columns - first_col
        owned = (local_col >= 0) & (local_col < column_width)
        position = obs_level[batch_index] * column_width + jnp.clip(local_col, 0, column_width - 1)
        picked = jnp.where(owned[None, :], jnp.take(flattened, position, axis=1), 0.0)
        obs_prior = lax.psum(picked, ("mem", "col"))
        obs_anom, weights = obs_weights(
            obs_prior, obs_value[batch_index], obs_variance[batch_index], members
        )
        anomalies = field_state - jnp.mean(field_state, axis=0)[None]
        for start in range(0, P_SIZE, obs_step):
            update = partial(
                apply_block,
                anom_part=obs_anom[:, start : start + obs_step],
                weight_part=weights[:, start : start + obs_step],
                col_part=columns[start : start + obs_step],
                anomalies=anomalies,
                first_col=first_col,
            )
            field_state = update(field_state)
    return to_owners(field_state)


def solution(mesh):
    return jax.shard_map(
        local,
        mesh=mesh,
        in_specs=(P("mem", "col", None), P(), P(), P(), P()),
        out_specs=P("mem", "col", None),
        check_vma=False,
    )
```

profile of v0, /device:TPU:0, one launch (start us, length us, event | category | flops | bytes accessed | tf_op | source)
XLA Modules:
  0.0 1034.5 jit_solution(4668524157783796177)
XLA Ops:
  6.5 11.7 %reshape.1220 = f32[20,4,16,2,768]{4,3,2,1,0:T(2,128)} reshape(f32[20,4,24576]{2,1,0:T(4,128)} %param.7) | data formatting | bytes 15728640 | tf_op jit(solution)/shard_map/reshape | solution.py:55
  18.3 4.2 copy.55
  22.5 8.3 copy.56
  30.8 7.4 all-to-all-start
  38.2 0.6 all-reduce.3.cloned.1.call-start
  38.8 0.0 copy-done.3
  38.8 0.0 copy-done.4
  39.0 6.5 fusion.75
  45.5 166.4 %all-to-all-done = f32[20,4,32,768]{3,1,0,2:T(4,128)} async-done(((f32[20,4,32,768]{3,1,0,2:T(4,128)}), f32[20,4,32,768]{3,1,0,2:T(4,128)}, u32[]{:S(2)}, u32[]{:S(2)}) %all-to-all-start) | async-done | bytes 7864352 | tf_op jit(solution)/shard_map/all_to_all | solution.py:77
  211.9 7.8 copy.101
  219.7 8.3 copy.58
  227.9 10.0 reshape.1223
  237.9 10.0 reshape_reshape.3
  247.9 7.3 fusion.128
  255.3 10.9 %copy.60 = f32[80,24576]{0,1:T(8,128)} copy(f32[80,24576]{1,0:T(8,128)} %reshape_reshape.3) | data formatting | bytes 15728640 | tf_op jit(solution)/shard_map/reshape;reshape | solution.py:127
  266.2 5.6 gather_fusion
  271.8 0.1 copy.61
  271.9 0.7 bitcast_select_fusion.1
  272.6 0.0 all-reduce.3.cloned.1.call-update
  272.6 0.0 all-reduce.5.cloned.1.call-start
  272.7 7.7 broadcast_subtract_fusion
  280.4 111.9 %all-reduce.3.cloned.1.call-done = f32[80,512]{1,0:T(8,128)} async-done(((f32[80,512]{1,0:T(8,128)}), f32[80,512]{1,0:T(8,128)}) %all-reduce.3.cloned.1.call-update) | async-done | bytes 163856 | tf_op jit(solution)/shard_map/psum | solution.py:133
  392.3 0.9 reduce_sum.54
  393.2 0.0 slice-start.2
  393.2 1.1 multiply_reduce_fusion.1
  394.3 20.9 %fusion.19 = f32[128,32,768]{2,0,1:T(8,128)} fusion(f32[80,32,768]{2,1,0:T(8,128)} %broadcast_subtract_fusion, f32[80,512]{1,0:T(8,128)S(1)} %get-tuple-element.11), kind=kOutput, calls=%fused_computation.26 | convolution fusion | flops 3019898880 | bytes 20488192 | tf_op jit(solution)/shard_map/kp,klc->plc/dot_general | solution.py:101
  415.3 0.0 slice-done.2
  415.3 0.0 slice-done.3
  415.3 16.3 %fusion.21 = f32[128,32,768]{2,0,1:T(8,128)} fusion(f32[80,32,768]{2,1,0:T(8,128)S(1)} %bitcast.160, f32[80,512]{1,0:T(8,128)S(1)} %get-tuple-element.11), kind=kOutput, calls=%fused_computation.28 | convolution fusion | flops 3019898880 | bytes 20488192 | tf_op jit(solution)/shard_map/kp,klc->plc/dot_general | solution.py:101
  431.6 15.3 %fusion.23 = f32[128,32,768]{2,0,1:T(8,128)S(1)} fusion(f32[80,32,768]{2,1,0:T(8,128)S(1)} %bitcast.160, f32[80,512]{1,0:T(8,128)S(1)} %get-tuple-element.11), kind=kOutput, calls=%fused_computation.30 | convolution fusion | flops 3019898880 | bytes 20488192 | tf_op jit(solution)/shard_map/kp,klc->plc/dot_general | solution.py:101
  446.9 0.0 copy-start.5
  446.9 0.0 copy-start.6
  446.9 0.0 copy-start.2
  446.9 15.9 %fusion.25 = f32[128,32,768]{2,0,1:T(8,128)} fusion(f32[80,32,768]{2,1,0:T(8,128)S(1)} %bitcast.160, f32[80,512]{1,0:T(8,128)S(1)} %get-tuple-element.11), kind=kOutput, calls=%fused_computation.32 | convolution fusion | flops 3019898880 | bytes 20488192 | tf_op jit(solution)/shard_map/kp,klc->plc/dot_general | solution.py:101
  462.9 0.0 copy-done.5
  462.9 0.0 copy-done.6
  463.0 13.1 %fusion.8 = f32[80,32,768]{2,0,1:T(8,128)} fusion(f32[128,32,768]{2,0,1:T(8,128)} %fusion.19, f32[128,768]{1,0:T(8,128)S(1)} %copy-done.2, f32[80,512]{1,0:T(8,128)S(1)} %multiply_subtract_fusion.1), kind=kOutput, calls=%fused_computation.10 | convolution fusion | flops 3023044608 | bytes 20881408 | tf_op jit(solution)/shard_map/kp,plc->klc/dot_general | solution.py:109
  476.0 13.3 %fusion.10 = f32[80,32,768]{2,0,1:T(8,128)} fusion(f32[128,32,768]{2,0,1:T(8,128)} %fusion.21, f32[128,768]{1,0:T(8,128)S(1)} %copy-done.1, f32[80,512]{1,0:T(8,128)S(1)} %multiply_subtract_fusion.1), kind=kOutput, calls=%fused_computation.12 | convolution fusion | flops 3023044608 | bytes 20881408 | tf_op jit(solution)/shard_map/kp,plc->klc/dot_general | solution.py:109
  489.3 10.3 fusion.12
  499.7 23.9 %fusion.129 = (f32[32,768]{1,0:T(8,128)S(1)}, f32[80,32,768]{2,0,1:T(8,128)}) fusion(f32[80,32,768]{2,0,1:T(8,128)} %fusion.8, f32[80,32,768]{2,0,1:T(8,128)} %fusion.10, f32[80,32,768]{2,0,1:T(8,128)} %fusion.12, f32[128,32,768]{2,0,1:T(8,128)} %fusion.25, f32[128,768]{1,0:T(8,128)S(1)} %get-tuple-element.19, f32[80,512]{1,0:T(8,128)S(1)} %multiply_subtract_fusion.1, ...), kind=kOutput, calls=%fused_computation.223 | convolution fusion | flops 3032850432 | bytes 52436992 | tf_op jit(solution)/shard_map/kp,plc->klc/dot_general | solution.py:109
  523.5 10.8 %copy.76 = f32[80,32,768]{0,2,1:T(8,128)} copy(f32[80,32,768]{2,0,1:T(8,128)} %get-tuple-element.43) | data formatting | bytes 15728640 | tf_op jit(solution)/shard_map/reshape | solution.py:127
  534.3 5.6 gather_fusion.1
  539.9 0.1 copy.70
  540.1 0.7 bitcast_select_fusion
  540.8 0.0 all-reduce.5.cloned.1.call-update
  540.8 124.0 %all-reduce.5.cloned.1.call-done = f32[80,512]{1,0:T(8,128)} async-done(((f32[80,512]{1,0:T(8,128)}), f32[80,512]{1,0:T(8,128)}) %all-reduce.5.cloned.1.call-update) | async-done | bytes 163856 | tf_op jit(solution)/shard_map/psum | solution.py:133
  664.8 0.9 reduce_sum.57
  665.7 1.0 multiply_reduce_fusion
  666.7 15.6 %fusion.27 = f32[128,32,768]{2,0,1:T(8,128)} fusion(f32[80,32,768]{2,0,1:T(8,128)} %get-tuple-element.43, f32[32,768]{1,0:T(8,128)S(1)} %broadcast_multiply_fusion, f32[80,512]{1,0:T(8,128)S(1)} %get-tuple-element.9), kind=kOutput, calls=%fused_computation.34 | convolution fusion | flops 3021864960 | bytes 20586496 | tf_op jit(solution)/shard_map/kp,klc->plc/dot_general | solution.py:101
  682.3 15.6 %fusion.29 = f32[128,32,768]{2,0,1:T(8,128)} fusion(f32[80,32,768]{2,0,1:T(8,128)} %get-tuple-element.43, f32[32,768]{1,0:T(8,128)S(1)} %broadcast_multiply_fusion, f32[80,512]{1,0:T(8,128)S(1)} %get-tuple-element.9), kind=kOutput, calls=%fused_computation.36 | convolution fusion | flops 3021864960 | bytes 20586496 | tf_op jit(solution)/shard_map/kp,klc->plc/dot_general | solution.py:101
  698.0 11.0 %fusion.31 = f32[128,32,768]{2,0,1:T(8,128)S(1)} fusion(f32[80,32,768]{2,0,1:T(8,128)S(1)} %bitcast.158, f32[32,768]{1,0:T(8,128)S(1)} %broadcast_multiply_fusion, f32[80,512]{1,0:T(8,128)S(1)} %get-tuple-element.9), kind=kOutput, calls=%fused_computation.38 | convolution fusion | flops 3021864960 | bytes 20586496 | tf_op jit(solution)/shard_map/kp,klc->plc/dot_general | solution.py:101
  708.9 13.1 %fusion.33 = f32[128,32,768]{2,0,1:T(8,128)} fusion(f32[80,32,768]{2,0,1:T(8,128)S(1)} %bitcast.158, f32[32,768]{1,0:T(8,128)S(1)} %broadcast_multiply_fusion, f32[80,512]{1,0:T(8,128)S(1)} %get-tuple-element.9), kind=kOutput, calls=%fused_computation.40 | convolution fusion | flops 3021864960 | bytes 20586496 | tf_op jit(solution)/shard_map/kp,klc->plc/dot_general | solution.py:101
  722.1 13.2 %fusion = f32[80,32,768]{2,0,1:T(8,128)} fusion(f32[128,32,768]{2,0,1:T(8,128)} %fusion.27, f32[128,768]{1,0:T(8,128)S(1)} %get-tuple-element.18, f32[80,512]{1,0:T(8,128)S(1)} %multiply_subtract_fusion), kind=kOutput, calls=%fused_computation.2 | convolution fusion | flops 3023044608 | bytes 20881408 | tf_op jit(solution)/shard_map/kp,plc->klc/dot_general | solution.py:109
  735.2 13.1 %fusion.2 = f32[80,32,768]{2,0,1:T(8,128)} fusion(f32[128,32,768]{2,0,1:T(8,128)} %fusion.29, f32[128,768]{1,0:T(8,128)S(1)} %get-tuple-element.17, f32[80,512]{1,0:T(8,128)S(1)} %multiply_subtract_fusion), kind=kOutput, calls=%fused_computation.4 | convolution fusion | flops 3023044608 | bytes 20881408 | tf_op jit(solution)/shard_map/kp,plc->klc/dot_general | solution.py:109
  748.4 10.5 %fusion.4 = f32[80,32,768]{2,0,1:T(8,128)} fusion(f32[128,32,768]{2,0,1:T(8,128)S(1)} %fusion.31, f32[128,768]{1,0:T(8,128)S(1)} %get-tuple-element.16, f32[80,512]{1,0:T(8,128)S(1)} %multiply_subtract_fusion), kind=kOutput, calls=%fused_computation.6 | convolution fusion | flops 3023044608 | bytes 20881408 | tf_op jit(solution)/shard_map/kp,plc->klc/dot_general | solution.py:109
  758.8 20.6 %add_add_fusion = f32[80,32,768]{2,0,1:T(8,128)} fusion(f32[80,32,768]{2,0,1:T(8,128)} %fusion, f32[80,32,768]{2,0,1:T(8,128)} %fusion.2, f32[80,32,768]{2,0,1:T(8,128)} %fusion.4, f32[80,32,768]{2,0,1:T(8,128)} %get-tuple-element.43, f32[128,32,768]{2,0,1:T(8,128)} %fusion.33, f32[128,768]{1,0:T(8,128)S(1)} %get-tuple-element.12, ...), kind=kOutput, calls=%fused_computation.25 | convolution fusion | flops 3030908928 | bytes 52338688 | tf_op jit(solution)/shard_map/kp,plc->klc/dot_general | solution.py:109
  779.5 9.3 reshape.1267
  788.8 12.0 %copy.99 = f32[4,20,8,4,768]{4,3,2,1,0:T(4,128)} copy(f32[4,20,8,4,768]{4,1,0,3,2:T(8,128)} %reshape.1267) | data formatting | bytes 15728640 | tf_op jit(solution)/shard_map/reshape | solution.py:90
  800.7 4.6 copy.100
  805.4 8.5 copy.73
  813.9 180.3 %all_to_all.10 = f32[20,4,32,768]{3,1,0,2:T(4,128)S(1)} all-to-all(f32[20,4,32,768]{3,1,0,2:T(4,128)} %copy.73), channel_id=1, replica_groups=mesh['mem'=4,'col'=8] {'mem','col'}, dimensions={2} | all-to-all | bytes 15728640 | tf_op jit(solution)/shard_map/all_to_all | solution.py:94
  994.2 7.8 copy.74
  1002.0 14.1 %copy.75 = f32[20,4,16,2,768]{4,3,2,1,0:T(2,128)} copy(f32[20,4,16,2,768]{4,2,3,1,0:T(8,128)} %bitcast.164) | data formatting | bytes 15728640 | tf_op jit(solution)/shard_map/transpose | solution.py:64
  1016.1 11.5 %reshape.1228 = f32[20,4,24576]{2,1,0:T(4,128)} reshape(f32[20,4,16,2,768]{4,3,2,1,0:T(2,128)} %copy.75) | data formatting | bytes 15728640 | tf_op jit(solution)/shard_map/reshape | solution.py:67
  (36 shorter events, 0.4 us)
Async XLA Ops:
  30.8 8.0 copy-start.3
  30.8 8.0 copy-start.4
  30.8 181.1 %all-to-all-start = ((f32[20,4,32,768]{3,1,0,2:T(4,128)}), f32[20,4,32,768]{3,1,0,2:T(4,128)}, u32[]{:S(2)}, u32[]{:S(2)}) async-start(f32[20,4,32,768]{3,1,0,2:T(4,128)} %copy.56), calls=%async_computation | async-start | bytes 15728640 | tf_op jit(solution)/shard_map/all_to_all | solution.py:77
  38.2 354.1 %all-reduce.3.cloned.1.call-start = ((), (), s32[]{:S(2)}) async-start(), calls=%async_computation.2 | async-start | bytes 327680 | tf_op jit(solution)/shard_map/psum | solution.py:133
  272.6 392.1 %all-reduce.5.cloned.1.call-start = ((), (), s32[]{:S(2)}) async-start(), calls=%async_computation.3 | async-start | bytes 327680 | tf_op jit(solution)/shard_map/psum | solution.py:133
  393.2 22.1 %slice-start.2 = ((s8[7864320]{0:T(1024)(128)(4,1)}), s8[4194304]{0:T(1024)(128)(4,1)S(1)}, s32[]{:S(2)}) async-start(s8[7864320]{0:T(1024)(128)(4,1)} %bitcast.159), calls=%async_computation.6 | async-start | bytes 8388608
  394.3 21.0 %slice-start.3 = ((s8[7864320]{0:T(1024)(128)(4,1)}), s8[3670016]{0:T(1024)(128)(4,1)S(1)}, s32[]{:S(2)}) async-start(s8[7864320]{0:T(1024)(128)(4,1)} %bitcast.159), calls=%async_computation.7 | async-start | bytes 7340032
  446.9 16.0 %copy-start.5 = (f32[2,512]{1,0:T(2,128)S(1)}, f32[2,512]{1,0:T(2,128)}, u32[]{:S(2)}) copy-start(f32[2,512]{1,0:T(2,128)} %param.10) | copy-start | bytes 12292
  446.9 16.0 %copy-start.6 = (f32[2,512]{1,0:T(2,128)S(1)}, f32[2,512]{1,0:T(2,128)}, u32[]{:S(2)}) copy-start(f32[2,512]{1,0:T(2,128)} %param.11) | copy-start | bytes 12292
  446.9 16.0 %copy-start.2 = (f32[128,768]{1,0:T(8,128)S(1)}, f32[128,768]{1,0:T(8,128)}, u32[]{:S(2)}) copy-start(f32[128,768]{1,0:T(8,128)} %get-tuple-element.15) | copy-start | bytes 1179652
  463.0 13.1 %copy-start.1 = (f32[128,768]{1,0:T(8,128)S(1)}, f32[128,768]{1,0:T(8,128)}, u32[]{:S(2)}) copy-start(f32[128,768]{1,0:T(8,128)} %get-tuple-element.14) | copy-start | bytes 1179652
  476.0 13.3 %copy-start = (f32[128,768]{1,0:T(8,128)S(1)}, f32[128,768]{1,0:T(8,128)}, u32[]{:S(2)}) copy-start(f32[128,768]{1,0:T(8,128)} %get-tuple-element.13) | copy-start | bytes 1179652
  666.7 31.3 %slice-start = ((s8[7864320]{0:T(1024)(128)(4,1)}), s8[4194304]{0:T(1024)(128)(4,1)S(1)}, s32[]{:S(2)}) async-start(s8[7864320]{0:T(1024)(128)(4,1)} %bitcast.157), calls=%async_computation.4 | async-start | bytes 8388608
  682.3 15.6 %slice-start.1 = ((s8[7864320]{0:T(1024)(128)(4,1)}), s8[3670016]{0:T(1024)(128)(4,1)S(1)}, s32[]{:S(2)}) async-start(s8[7864320]{0:T(1024)(128)(4,1)} %bitcast.157), calls=%async_computation.5 | async-start | bytes 7340032
Sparse Core Ops, SparseCore 0:
  272.8 119.4 all-reduce.2
  540.9 123.8 all-reduce.4
where the time goes:
time: 1040 us; the launch traced here: 1030 us
  waiting for transfers between devices  402 us (39%)
  matrix products  242 us (23%)
  blocking collectives  180 us (17%)
  local copies, waits for them, and re-layouts  161 us (15%)
  other arithmetic  27.1 us (3%)
  between operations  13.9 us (1%)
    psum x2, waiting for transfers between devices, local(): obs_prior = lax.psum(picked, ('mem', 'col'))  236 us
    all_to_all x1, blocking collectives, to_owners(): lax.all_to_all(outgoing, ('mem', 'col'), split_axis=2, concat_axis=2, til...  180 us
    all_to_all x1, waiting for transfers between devices, to_tiles(): lax.all_to_all(outgoing, ('mem', 'col'), split_axis=2, concat_axis=2, til...  166 us
    dot_general x8, matrix products, apply_block(): jnp.einsum('kp,klc->plc', anom_part, anomalies, precision=lax.Precision.H...  124 us
    dot_general x8, matrix products, apply_block(): jnp.einsum('kp,plc->klc', weight_part, gain_block, precision=lax.Precisio...  118 us
    reshape x2, local copies, waits for them, and re-layouts, to_owners(): field_state.reshape(mem_count, own_members, col_count, own_levels, column...  21.2 us
    another operation x2, local copies, waits for them, and re-layouts, local(): flattened = field_state.reshape(members, levels * column_width)  20.9 us
  transfers between devices with their start and end apart: 3, of which 3 were waited for; matrix products, arithmetic and copies ran while one was open for 1% of the time, Pallas kernels for 0%

commit v1 on v0

v1 whole, which is shorter than its diff:
```python
import functools

import jax
import jax.numpy as jnp
from jax import lax
from jax.experimental import pallas as pl
from jax.experimental.pallas import tpu as pltpu
from jax.sharding import PartitionSpec as P

NLON = 768
P_SIZE = 512
NB = 2
LOCR = 6
REACH = 2 * LOCR
LANES = 128
BLOCKS = NLON // LANES
CHUNK = 80
CHUNKS = -(-P_SIZE // CHUNK)
PADDED = CHUNK * CHUNKS
SLABS = 4
GROUP = 4
MESH = pl.DeviceIdType.MESH


def gc_taper(squared_gap):
    scaled = jnp.sqrt(squared_gap) * (1.0 / LOCR)
    near_part = (
        ((-0.25 * scaled + 0.5) * scaled + 0.625) * scaled - 5.0 / 3.0
    ) * scaled * scaled + 1.0
    bounded = jnp.maximum(scaled, 1.0)
    far_part = (
        ((((scaled / 12.0 - 0.5) * scaled + 0.625) * scaled + 5.0 / 3.0) * scaled - 5.0) * scaled
        + 4.0
        - 2.0 / (3.0 * bounded)
    )
    return jnp.where(
        squared_gap < LOCR * LOCR,
        near_part,
        jnp.where(squared_gap < 4 * LOCR * LOCR, far_part, 0.0),
    )


def taper_of(rows, lons, obs_rows, obs_lons):
    row_gap = rows - obs_rows
    lon_gap = jnp.abs(lons - obs_lons)
    lon_gap = jnp.minimum(lon_gap, NLON - lon_gap)
    return gc_taper(row_gap * row_gap + lon_gap * lon_gap)


def obs_weights(picked, values, variances):
    members = picked.shape[0]
    obs_mean = jnp.mean(picked, axis=0)
    obs_anom = picked - obs_mean[None, :]
    obs_total = jnp.sum(obs_anom * obs_anom, axis=0) / (members - 1) + variances
    mean_gain = (values - obs_mean) / obs_total
    root_gain = 1.0 / (obs_total * (1.0 + jnp.sqrt(variances / obs_total)))
    weights = mean_gain[None, :] - root_gain[None, :] * obs_anom
    return (obs_anom, weights)


def split(x):
    high = x.astype(jnp.bfloat16)
    low = (x - high.astype(jnp.float32)).astype(jnp.bfloat16)
    return high, low


def split_outside(x):
    high = lax.reduce_precision(x, exponent_bits=8, mantissa_bits=7)
    return high.astype(jnp.bfloat16), (x - high).astype(jnp.bfloat16)


def exchange_in_kernel(mem_n, col_n, prior, picked, tile, obs, slots, total, sends, recvs, own, psend, precv, osend, orecv):
    m = lax.axis_index("mem")
    c = lax.axis_index("col")
    rows = prior.shape[1]
    tiles = tile.shape[0]
    here = pl.ds(pl.multiple_of(m * rows, 8), rows)
    barrier = pltpu.get_barrier_semaphore()
    for j in range(1, mem_n):
        pl.semaphore_signal(barrier, inc=1, device_id=(lax.rem(m + j, mem_n), c), device_id_type=MESH)
    for j in range(1, col_n):
        pl.semaphore_signal(barrier, inc=1, device_id=(m, lax.rem(c + j, col_n)), device_id_type=MESH)
    pl.semaphore_wait(barrier, mem_n + col_n - 2)

    picks = []
    for j in range(1, col_n):
        copy = pltpu.make_async_remote_copy(
            src_ref=picked,
            dst_ref=slots.at[j],
            send_sem=psend.at[j],
            recv_sem=precv.at[j],
            device_id=(m, lax.rem(c + j, col_n)),
            device_id_type=MESH,
        )
        copy.start()
        picks.append(copy)
    bulk = []
    for j in range(1, mem_n):
        q = lax.rem(m + j, mem_n)
        copy = pltpu.make_async_remote_copy(
            src_ref=prior.at[pl.ds(q * tiles, tiles)],
            dst_ref=tile.at[:, here],
            send_sem=sends.at[j],
            recv_sem=recvs.at[j],
            device_id=(q, c),
            device_id_type=MESH,
        )
        copy.start()
        bulk.append(copy)
    mine = pltpu.make_async_copy(prior.at[pl.ds(m * tiles, tiles)], tile.at[:, here], own)
    mine.start()
    for copy in picks:
        copy.wait_recv()
    summed = picked[...]
    for j in range(1, col_n):
        summed = summed + slots[j]
    total[...] = summed
    obs[m] = summed
    shares = []
    for j in range(1, mem_n):
        copy = pltpu.make_async_remote_copy(
            src_ref=total,
            dst_ref=obs.at[m],
            send_sem=osend.at[j],
            recv_sem=orecv.at[j],
            device_id=(lax.rem(m + j, mem_n), c),
            device_id_type=MESH,
        )
        copy.start()
        shares.append(copy)
    for copy in shares:
        copy.wait()
    for copy in picks:
        copy.wait_send()
    for copy in bulk:
        copy.wait()
    mine.wait()


def exchange_in(prior, picked, mem_n, col_n):
    tiles, rows, lanes = prior.shape
    return pl.pallas_call(
        functools.partial(exchange_in_kernel, mem_n, col_n),
        out_shape=(
            jax.ShapeDtypeStruct((tiles // mem_n, rows * mem_n, lanes), jnp.float32),
            jax.ShapeDtypeStruct((mem_n,) + picked.shape, jnp.float32),
        ),
        in_specs=[pl.BlockSpec(memory_space=pl.ANY), pl.BlockSpec(memory_space=pltpu.VMEM)],
        out_specs=(pl.BlockSpec(memory_space=pl.ANY), pl.BlockSpec(memory_space=pltpu.VMEM)),
        scratch_shapes=[
            pltpu.VMEM((col_n,) + picked.shape, jnp.float32),
            pltpu.VMEM(picked.shape, jnp.float32),
            pltpu.SemaphoreType.DMA((mem_n,)),
            pltpu.SemaphoreType.DMA((mem_n,)),
            pltpu.SemaphoreType.DMA,
            pltpu.SemaphoreType.DMA((col_n,)),
            pltpu.SemaphoreType.DMA((col_n,)),
            pltpu.SemaphoreType.DMA((mem_n,)),
            pltpu.SemaphoreType.DMA((mem_n,)),
        ],
        compiler_params=pltpu.CompilerParams(collective_id=0, has_side_effects=True),
        name="exchange_in",
    )(prior, picked)


def exchange_out_kernel(mem_n, tile, out, sends, recvs, own):
    m = lax.axis_index("mem")
    c = lax.axis_index("col")
    rows = out.shape[1]
    tiles = tile.shape[0]
    barrier = pltpu.get_barrier_semaphore()
    for j in range(1, mem_n):
        pl.semaphore_signal(barrier, inc=1, device_id=(lax.rem(m + j, mem_n), c), device_id_type=MESH)
    pl.semaphore_wait(barrier, mem_n - 1)
    bulk = []
    place = pl.ds(m * tiles, tiles)
    for j in range(1, mem_n):
        q = lax.rem(m + j, mem_n)
        copy = pltpu.make_async_remote_copy(
            src_ref=tile.at[:, pl.ds(pl.multiple_of(q * rows, 8), rows)],
            dst_ref=out.at[place],
            send_sem=sends.at[j],
            recv_sem=recvs.at[j],
            device_id=(q, c),
            device_id_type=MESH,
        )
        copy.start()
        bulk.append(copy)
    mine = pltpu.make_async_copy(
        tile.at[:, pl.ds(pl.multiple_of(m * rows, 8), rows)], out.at[place], own
    )
    mine.start()
    for copy in bulk:
        copy.wait()
    mine.wait()


def exchange_out(tile, mem_n):
    tiles, all_rows, lanes = tile.shape
    return pl.pallas_call(
        functools.partial(exchange_out_kernel, mem_n),
        out_shape=jax.ShapeDtypeStruct((tiles * mem_n, all_rows // mem_n, lanes), jnp.float32),
        in_specs=[pl.BlockSpec(memory_space=pl.ANY)],
        out_specs=pl.BlockSpec(memory_space=pl.ANY),
        scratch_shapes=[
            pltpu.SemaphoreType.DMA((mem_n,)),
            pltpu.SemaphoreType.DMA((mem_n,)),
            pltpu.SemaphoreType.DMA,
        ],
        compiler_params=pltpu.CompilerParams(collective_id=1, has_side_effects=True),
        name="exchange_out",
    )(tile)


def update_kernel(members, shared, near, first_row, tile, anom, weight, obs_row, obs_lon, out, current, spread):
    groups = tile.shape[0] // (BLOCKS * GROUP)
    span = GROUP * LANES
    lane = lax.broadcasted_iota(jnp.int32, (1, LANES), 1)

    def step(index, carry):
        block = index // groups
        group = lax.rem(index, groups)
        starts = [(group * GROUP + r) * BLOCKS + block for r in range(GROUP)]
        for s in range(SLABS):
            for r in range(GROUP):
                at = s * span + r * LANES
                current[:, at : at + LANES] = tile[starts[r], pl.ds(s, members, stride=SLABS), :]
        lons = (block * LANES + lane).astype(jnp.float32)
        for b in range(NB):
            for s in range(SLABS):
                part = current[:, s * span : (s + 1) * span]
                high, low = split(part - jnp.mean(part, axis=0, keepdims=True))
                spread[:, s * span : (s + 1) * span] = jnp.concatenate([high, low, high], axis=0)
            for chunk in range(CHUNKS):

                @pl.when(near[b, chunk, block] != 0)
                def _():
                    here = pl.ds(chunk * CHUNK, CHUNK)
                    rows_here = obs_row[b, here, :]
                    lons_here = obs_lon[b, here, :]
                    gains = None
                    for s in range(SLABS):
                        if s == 0 or not shared:
                            gains = jnp.concatenate(
                                [
                                    taper_of(
                                        (first_row[s] + group * GROUP + r).astype(jnp.float32),
                                        lons,
                                        rows_here,
                                        lons_here,
                                    )
                                    for r in range(GROUP)
                                ],
                                axis=1,
                            )
                        cov = jnp.dot(
                            anom[b, here, :],
                            spread[:, s * span : (s + 1) * span],
                            preferred_element_type=jnp.float32,
                        )
                        high, low = split(cov * gains)
                        current[:, s * span : (s + 1) * span] += jnp.dot(
                            weight[b, chunk],
                            jnp.concatenate([high, low, high], axis=0),
                            preferred_element_type=jnp.float32,
                        )
        for s in range(SLABS):
            for r in range(GROUP):
                at = s * span + r * LANES
                out[starts[r], pl.ds(s, members, stride=SLABS), :] = current[:, at : at + LANES]
        return carry

    lax.fori_loop(0, BLOCKS * groups, step, 0)


def update(tile, near, first_row, anom, weight, obs_row, obs_lon, shared):
    members = tile.shape[1] // SLABS
    whole = pl.BlockSpec(memory_space=pltpu.VMEM)
    scalars = pl.BlockSpec(memory_space=pltpu.SMEM)
    return pl.pallas_call(
        functools.partial(update_kernel, members, shared),
        out_shape=jax.ShapeDtypeStruct(tile.shape, jnp.float32),
        in_specs=[scalars, scalars, whole, whole, whole, whole, whole],
        out_specs=whole,
        scratch_shapes=[
            pltpu.VMEM((members, SLABS * GROUP * LANES), jnp.float32),
            pltpu.VMEM((3 * members, SLABS * GROUP * LANES), jnp.bfloat16),
        ],
        compiler_params=pltpu.CompilerParams(vmem_limit_bytes=40 * 1024 * 1024),
        name="update",
    )(near, first_row, tile, anom, weight, obs_row, obs_lon)


def by_longitude(columns, arrays):
    lons = columns % NLON
    count = columns.shape[1]
    index = jnp.arange(count, dtype=jnp.int32)
    before = (lons[:, :, None] < lons[:, None, :]) | (
        (lons[:, :, None] == lons[:, None, :]) & (index[:, None] < index[None, :])[None]
    )
    rank = jnp.sum(before.astype(jnp.int32), axis=1)
    chosen = rank[:, :, None] == index[None, None, :]
    return [jnp.sum(jnp.where(chosen, a[:, :, None], jnp.zeros((), a.dtype)), axis=1) for a in arrays]


def near_blocks(columns):
    lons = columns % NLON
    past = (lons[:, :, None] - (jnp.arange(BLOCKS, dtype=jnp.int32) * LANES)[None, None, :]) % NLON
    hit = (past < LANES + REACH) | (past > NLON - REACH)
    hit = jnp.pad(hit, ((0, 0), (0, PADDED - P_SIZE), (0, 0)))
    return jnp.any(hit.reshape(NB, CHUNKS, CHUNK, BLOCKS), axis=2).astype(jnp.int32)


def local(prior, obs_column, obs_level, obs_value, obs_variance):
    own_members, own_levels, all_columns = prior.shape
    mem_n = lax.axis_size("mem")
    col_n = lax.axis_size("col")
    m = lax.axis_index("mem")
    c = lax.axis_index("col")
    members = own_members * mem_n
    parts = SLABS // own_levels
    part_columns = all_columns // parts
    width = part_columns // mem_n
    tiles = part_columns // LANES
    prior = prior.reshape(own_members, SLABS, part_columns)

    columns, levels, values, variances = by_longitude(
        obs_column, [obs_column, obs_level, obs_value, obs_variance]
    )

    flat_column = columns.reshape(-1)
    flat_level = levels.reshape(-1)
    slab = (flat_level % own_levels) * parts + flat_column // part_columns
    owned = flat_level // own_levels == c
    picked = jnp.take(prior, flat_column % part_columns, axis=2)
    mine = (slab[None, :] == jnp.arange(SLABS, dtype=jnp.int32)[:, None]) & owned[None, :]
    picked = jnp.sum(jnp.where(mine[None], picked, 0.0), axis=1)
    picked = jnp.pad(picked, ((0, -own_members % 8), (0, 0)))

    prior = prior.reshape(own_members, SLABS, tiles, LANES).transpose(2, 0, 1, 3)
    prior = prior.reshape(tiles, own_members * SLABS, LANES)
    tile, obs = exchange_in(prior, picked, mem_n, col_n)
    obs = obs[:, :own_members].reshape(members, NB, P_SIZE)

    rows = (columns // NLON).astype(jnp.float32)
    lons = (columns % NLON).astype(jnp.float32)
    scale = 1.0 / (members - 1)
    state = [obs[:, b] for b in range(NB)]
    anoms, weights = [], []
    for b in range(NB):
        obs_anom, weight = obs_weights(state[b], values[b], variances[b])
        anoms.append(obs_anom * scale)
        weights.append(weight)
        for later in range(b + 1, NB):
            anomalies = state[later] - jnp.mean(state[later], axis=0)[None]
            cov = jnp.einsum(
                "kp,kc->pc",
                obs_anom * scale,
                anomalies,
                precision=lax.Precision.HIGHEST,
                preferred_element_type=jnp.float32,
            )
            gain = cov * taper_of(
                rows[later][None, :], lons[later][None, :], rows[b][:, None], lons[b][:, None]
            )
            state[later] = state[later] + jnp.einsum(
                "kp,pc->kc",
                weight,
                gain,
                precision=lax.Precision.HIGHEST,
                preferred_element_type=jnp.float32,
            )

    extra = PADDED - P_SIZE
    high, low = split_outside(jnp.stack(anoms).transpose(0, 2, 1))
    anom = jnp.pad(jnp.concatenate([high, high, low], axis=2), ((0, 0), (0, extra), (0, 0)))
    weight = jnp.pad(jnp.stack(weights), ((0, 0), (0, 0), (0, extra)))
    weight = weight.reshape(NB, members, CHUNKS, CHUNK).transpose(0, 2, 1, 3)
    high, low = split_outside(weight)
    weight = jnp.concatenate([high, high, low], axis=3)
    obs_row = jnp.pad(rows, ((0, 0), (0, extra)))[:, :, None]
    obs_lon = jnp.pad(lons, ((0, 0), (0, extra)))[:, :, None]

    slabs = jnp.arange(SLABS, dtype=jnp.int32)
    first_row = ((slabs % parts) * part_columns + m * width) // NLON
    done = update(
        tile, near_blocks(columns), first_row, anom, weight, obs_row, obs_lon, parts == 1
    )
    out = exchange_out(done, mem_n).reshape(tiles, own_members, SLABS, LANES)
    out = out.transpose(1, 2, 0, 3)
    return out.reshape(own_members, own_levels, all_columns)


def solution(mesh):
    return jax.shard_map(
        local,
        mesh=mesh,
        in_specs=(P("mem", "col", None), P(), P(), P(), P()),
        out_specs=P("mem", "col", None),
        check_vma=False,
    )
```

time: 1040 us -> 354 us (0.34)
  waiting for transfers between devices: 402 us -> 0 us
  Pallas kernels: 0 us -> 262 us
  matrix products: 242 us -> 4.65 us
  blocking collectives: 180 us -> 0 us
  local copies, waits for them, and re-layouts: 161 us -> 70.2 us
  other arithmetic: 27.1 us -> 12.5 us
  between operations: 13.9 us -> 0.38 us
    pallas_call x0 -> x3, Pallas kernels: none -> 262 us  [the longest x1 98.3 us: exchange_in(): pl.pallas_call(functools.partial(exchange_in_kernel, mem_n, col_n), out_s...]
    dot_general x16 -> x2, matrix products: 242 us -> 4.65 us  [the longest x1 2.54 us: local(): jnp.einsum('kp,kc->pc', obs_anom * scale, anomalies, precision=lax.Precis...]
    psum x2 -> x0, waiting for transfers between devices: 236 us -> none  [local(): obs_prior = lax.psum(picked, ('mem', 'col'))]
    all_to_all x1 -> x0, blocking collectives: 180 us -> none  [to_owners(): lax.all_to_all(outgoing, ('mem', 'col'), split_axis=2, concat_axis=2, til...]
    all_to_all x1 -> x0, waiting for transfers between devices: 166 us -> none  [to_tiles(): lax.all_to_all(outgoing, ('mem', 'col'), split_axis=2, concat_axis=2, til...]
    reshape x8 -> x5, local copies, waits for them, and re-layouts: 82 us -> 17.9 us  [the longest x1 8.56 us: local(): return out.reshape(own_members, own_levels, all_columns)]
    unnamed x22 -> x13, local copies, waits for them, and re-layouts: 0.05 us -> 39.1 us
    transpose x4 -> x0, local copies, waits for them, and re-layouts: 31.3 us -> none  [the longest x1 14.1 us: unpair_blocks(): field.reshape(own_members, own_levels, 2, halves, column_width)]
  transfers between devices with their start and end apart: 3 -> 0, of which waited for: 3 -> 0; matrix products, arithmetic and copies ran while one was open for 1% -> 0% of each run, Pallas kernels for 0% -> 0%
where the time goes in v1:
time: 354 us; the launch traced here: 350 us
  Pallas kernels  262 us (74%)
  local copies, waits for them, and re-layouts  70.2 us (20%)
  other arithmetic  12.5 us (4%)
  matrix products  4.65 us (1%)
    pallas_call x1, Pallas kernels, exchange_in(): pl.pallas_call(functools.partial(exchange_in_kernel, mem_n, col_n), out_s...  98.3 us
    pallas_call x1, Pallas kernels, exchange_out(): pl.pallas_call(functools.partial(exchange_out_kernel, mem_n), out_shape=j...  87.9 us
    pallas_call x1, Pallas kernels, update(): pl.pallas_call(functools.partial(update_kernel, members, shared), out_sha...  75.9 us
    unnamed x13, local copies, waits for them, and re-layouts  39.1 us
    gather x1, local copies, waits for them, and re-layouts, local(): picked = jnp.take(prior, flat_column % part_columns, axis=2)  11.7 us
    reshape x1, local copies, waits for them, and re-layouts, local(): return out.reshape(own_members, own_levels, all_columns)  8.56 us
    reshape x1, local copies, waits for them, and re-layouts, local(): prior.reshape(own_members, SLABS, tiles, LANES).transpose(2, 0, 1, 3)  7.8 us

profile of v1, /device:TPU:0, one launch (start us, length us, event | category | flops | bytes accessed | tf_op | source)
XLA Modules:
  0.0 349.8 jit_solution(11173390317887002641)
XLA Ops:
  0.0 0.1 iota_compare_fusion.2
  0.1 0.7 and_select_fusion.3
  0.8 0.6 convert_reduce_fusion
  1.4 1.3 select_reduce_fusion.2
  2.8 0.3 fusion.15
  3.2 35.6 %copy.43 = f32[20,4,24576]{0,1,2:T(4,128)} copy(f32[20,4,24576]{2,1,0:T(4,128)} %param.5) | data formatting | bytes 15728640 | tf_op args[0]
  38.8 11.7 %gather_fusion = f32[1024,20,4]{1,2,0:T(4,128)S(1)} fusion(f32[20,4,24576]{0,1,2:T(4,128)} %copy.43, s32[1024]{0:T(1024)S(1)} %broadcast_clamp_fusion), kind=kCustom, calls=%fused_computation | custom fusion | bytes 659456 | tf_op jit(solution)/shard_map/jit(_take)/gather | solution.py:335
  50.5 5.9 %fusion = f32[20,1024]{0,1:T(8,128)S(1)} fusion(f32[1024,20,4]{1,2,0:T(4,128)S(1)} %gather_fusion, pred[1024]{0:T(1024)(128)(4,1)S(1)} %compare_and_fusion, pred[4,1024]{0,1:T(8,128)(4,1)S(1)} %fusion.15), kind=kLoop, calls=%fused_computation.4 | loop fusion | flops 225280 | bytes 414720 | tf_op jit(solution)/shard_map/reduce_sum | solution.py:337
  56.4 0.2 copy.44
  56.6 0.7 pad.24.picked
  57.2 7.8 %copy_bitcast_fusion.1 = f32[20,4,192,128]{3,1,0,2:T(4,128)} fusion(f32[20,4,24576]{2,1,0:T(4,128)} %param.5), kind=kLoop, calls=%fused_computation.2 | loop fusion | bytes 15728640 | tf_op jit(solution)/shard_map/reshape | solution.py:340
  65.0 98.3 %exchange_in.1 = (f32[48,320,128]{2,1,0:T(8,128)}, f32[4,24,1024]{2,1,0:T(8,128)}) custom-call(f32[192,80,128]{2,1,0:T(8,128)} %bitcast.90, f32[24,1024]{1,0:T(8,128)} %pad.24.picked), custom_call_target="tpu_custom_call" | custom-call | tf_op jit(solution)/shard_map/exchange_in/pallas_call | solution.py:142
  163.3 0.0 copy-start.1
  163.3 0.0 copy-start.2
  163.3 1.3 reshape.385
  164.6 0.4 slice_reduce_fusion.1
  165.0 0.1 copy.56
  165.1 0.2 multiply_reduce_fusion.1
  165.4 0.0 copy-done.1
  165.4 0.0 copy-done.2
  165.4 0.8 select_reduce_fusion.1
  166.2 0.3 multiply_subtract_fusion
  166.5 0.1 copy.57
  166.7 2.5 convolution_multiply_fusion
  169.2 2.1 fusion.47
  171.3 0.2 multiply_reduce_fusion
  171.6 0.3 subtract_bitcast_fusion
  171.9 0.1 select_maximum_fusion
  172.0 0.2 copy.49
  172.2 0.1 reduce-precision_convert_fusion
  172.3 0.4 pad_maximum_fusion.weight
  172.6 0.1 reduce-precision_convert_fusion.1
  172.7 0.3 fusion.13.anom
  173.1 0.2 copy.50.obs_row
  173.3 0.2 copy.51.obs_lon
  173.6 0.1 fusion.34
  173.7 0.1 reshape.381
  173.8 0.3 reduce_or.9
  174.1 0.1 copy.41
  174.2 75.9 %update.1.tile = f32[48,320,128]{2,1,0:T(8,128)S(1)} custom-call(s32[2,7,6]{2,1,0:T(8,128)S(1)} %convert_element_type.36.near, s32[4]{0:T(128)S(1)} %add.154.first_row, f32[48,320,128]{2,1,0:T(8,128)} %get-tuple-element.7.tile, bf16[2,560,240]{2,1,0:T(8,128)(2,1)S(1)} %fusion.13.anom, bf16[2,7,80,240]{3,2,1,0:T(8,128)(2,1)S(1)} %pad_maximum_fusion.weight, ...), custom_call_target="tpu_custom_call" | custom-call | tf_op jit(solution)/shard_map/update/pallas_call | solution.py:280
  250.1 0.0 copy-start
  250.1 3.2 copy-done
  253.3 87.9 %exchange_out.1 = f32[192,80,128]{2,1,0:T(8,128)} custom-call(f32[48,320,128]{2,1,0:T(8,128)} %copy-done), custom_call_target="tpu_custom_call" | custom-call | tf_op jit(solution)/shard_map/exchange_out/pallas_call | solution.py:200
  341.3 8.6 %copy.68 = f32[192,20,1,4,128]{4,3,0,2,1:T(4,128)} copy(f32[192,20,1,4,128]{4,3,2,1,0:T(4,128)} %bitcast.91) | data formatting | bytes 15728640 | tf_op jit(solution)/shard_map/reshape | solution.py:391
  (24 shorter events, 0.2 us)
Async XLA Ops:
  163.3 2.1 copy-start.1
  163.3 2.1 copy-start.2
  250.1 3.2 copy-start

commit v2 on v1

--- a/solution.py
+++ b/solution.py
@@ -19,6 +19,7 @@
 PADDED = CHUNK * CHUNKS
 SLABS = 4
 GROUP = 4
+HALVES = 2
 MESH = pl.DeviceIdType.MESH
 
 
@@ -69,12 +70,44 @@
     return high.astype(jnp.bfloat16), (x - high).astype(jnp.bfloat16)
 
 
-def exchange_in_kernel(mem_n, col_n, prior, picked, tile, obs, slots, total, sends, recvs, own, psend, precv, osend, orecv):
+def pick_kernel(own_members, row, lane, owned, prior, out):
+    stride = prior.shape[0] // own_members
+    lanes = lax.broadcasted_iota(jnp.int32, (1, LANES), 1)
+
+    def block(i, carry):
+        def one(j, total):
+            at = i * LANES + j
+            values = prior[pl.ds(row[at], own_members, stride=stride), :]
+            turned = pltpu.roll(values, lax.rem(j - lane[at] + LANES, LANES), 1)
+            return jnp.where(lanes == jnp.where(owned[at] != 0, j, -1), turned, total)
+
+        total = lax.fori_loop(0, LANES, one, jnp.zeros((own_members, LANES), jnp.float32), unroll=8)
+        out[i, :own_members, :] = total
+        return carry
+
+    out[...] = jnp.zeros_like(out)
+    lax.fori_loop(0, out.shape[0], block, 0)
+
+
+def pick(prior, row, lane, owned, own_members):
+    scalars = pl.BlockSpec(memory_space=pltpu.SMEM)
+    blocks = row.shape[0] // LANES
+    return pl.pallas_call(
+        functools.partial(pick_kernel, own_members),
+        out_shape=jax.ShapeDtypeStruct(
+            (blocks, own_members + -own_members % 8, LANES), jnp.float32
+        ),
+        in_specs=[scalars, scalars, scalars, pl.BlockSpec(memory_space=pltpu.VMEM)],
+        out_specs=pl.BlockSpec(memory_space=pltpu.VMEM),
+        compiler_params=pltpu.CompilerParams(vmem_limit_bytes=16 * 1024 * 1024),
+        cost_estimate=pl.CostEstimate(flops=10**10, bytes_accessed=10**7, transcendentals=0),
+        name="pick",
+    )(row, lane, owned, prior)
+
+
+def gather_kernel(mem_n, col_n, picked, obs, slots, total, psend, precv, osend, orecv):
     m = lax.axis_index("mem")
     c = lax.axis_index("col")
-    rows = prior.shape[1]
-    tiles = tile.shape[0]
-    here = pl.ds(pl.multiple_of(m * rows, 8), rows)
     barrier = pltpu.get_barrier_semaphore()
     for j in range(1, mem_n):
         pl.semaphore_signal(barrier, inc=1, device_id=(lax.rem(m + j, mem_n), c), device_id_type=MESH)
@@ -94,21 +127,6 @@
         )
         copy.start()
         picks.append(copy)
-    bulk = []
-    for j in range(1, mem_n):
-        q = lax.rem(m + j, mem_n)
-        copy = pltpu.make_async_remote_copy(
-            src_ref=prior.at[pl.ds(q * tiles, tiles)],
-            dst_ref=tile.at[:, here],
-            send_sem=sends.at[j],
-            recv_sem=recvs.at[j],
-            device_id=(q, c),
-            device_id_type=MESH,
-        )
-        copy.start()
-        bulk.append(copy)
-    mine = pltpu.make_async_copy(prior.at[pl.ds(m * tiles, tiles)], tile.at[:, here], own)
-    mine.start()
     for copy in picks:
         copy.wait_recv()
     summed = picked[...]
@@ -132,99 +150,85 @@
         copy.wait()
     for copy in picks:
         copy.wait_send()
-    for copy in bulk:
-        copy.wait()
-    mine.wait()
-
-
-def exchange_in(prior, picked, mem_n, col_n):
-    tiles, rows, lanes = prior.shape
+
+
+def gather(picked, mem_n, col_n):
     return pl.pallas_call(
-        functools.partial(exchange_in_kernel, mem_n, col_n),
-        out_shape=(
-            jax.ShapeDtypeStruct((tiles // mem_n, rows * mem_n, lanes), jnp.float32),
-            jax.ShapeDtypeStruct((mem_n,) + picked.shape, jnp.float32),
-        ),
-        in_specs=[pl.BlockSpec(memory_space=pl.ANY), pl.BlockSpec(memory_space=pltpu.VMEM)],
-        out_specs=(pl.BlockSpec(memory_space=pl.ANY), pl.BlockSpec(memory_space=pltpu.VMEM)),
+        functools.partial(gather_kernel, mem_n, col_n),
+        out_shape=jax.ShapeDtypeStruct((mem_n,) + picked.shape, jnp.float32),
+        in_specs=[pl.BlockSpec(memory_space=pltpu.VMEM)],
+        out_specs=pl.BlockSpec(memory_space=pltpu.VMEM),
         scratch_shapes=[
             pltpu.VMEM((col_n,) + picked.shape, jnp.float32),
             pltpu.VMEM(picked.shape, jnp.float32),
-            pltpu.SemaphoreType.DMA((mem_n,)),
-            pltpu.SemaphoreType.DMA((mem_n,)),
-            pltpu.SemaphoreType.DMA,
             pltpu.SemaphoreType.DMA((col_n,)),
             pltpu.SemaphoreType.DMA((col_n,)),
             pltpu.SemaphoreType.DMA((mem_n,)),
             pltpu.SemaphoreType.DMA((mem_n,)),
         ],
         compiler_params=pltpu.CompilerParams(collective_id=0, has_side_effects=True),
-        name="exchange_in",
-    )(prior, picked)
-
-
-def exchange_out_kernel(mem_n, tile, out, sends, recvs, own):
+        cost_estimate=pl.CostEstimate(flops=2 * 10**10, bytes_accessed=10**6, transcendentals=0),
+        name="gather",
+    )(picked)
+
+
+def join_kernel(mem_n, *refs):
+    pieces, out, sems = refs[:-2], refs[-2], refs[-1]
     m = lax.axis_index("mem")
-    c = lax.axis_index("col")
-    rows = out.shape[1]
-    tiles = tile.shape[0]
-    barrier = pltpu.get_barrier_semaphore()
-    for j in range(1, mem_n):
-        pl.semaphore_signal(barrier, inc=1, device_id=(lax.rem(m + j, mem_n), c), device_id_type=MESH)
-    pl.semaphore_wait(barrier, mem_n - 1)
-    bulk = []
-    place = pl.ds(m * tiles, tiles)
-    for j in range(1, mem_n):
-        q = lax.rem(m + j, mem_n)
-        copy = pltpu.make_async_remote_copy(
-            src_ref=tile.at[:, pl.ds(pl.multiple_of(q * rows, 8), rows)],
-            dst_ref=out.at[place],
-            send_sem=sends.at[j],
-            recv_sem=recvs.at[j],
-            device_id=(q, c),
-            device_id_type=MESH,
+    rows = pieces[0].shape[1]
+    copies = []
+    for i, piece in enumerate(pieces):
+        half, j = divmod(i, mem_n)
+        at = (jnp.bitwise_xor(m, j) * HALVES + half) * rows
+        copy = pltpu.make_async_copy(
+            piece, out.at[:, pl.ds(pl.multiple_of(at, 8), rows)], sems.at[i]
         )
         copy.start()
-        bulk.append(copy)
-    mine = pltpu.make_async_copy(
-        tile.at[:, pl.ds(pl.multiple_of(m * rows, 8), rows)], out.at[place], own
-    )
-    mine.start()
-    for copy in bulk:
+        copies.append(copy)
+    for copy in copies:
         copy.wait()
-    mine.wait()
-
-
-def exchange_out(tile, mem_n):
-    tiles, all_rows, lanes = tile.shape
+
+
+def join(pieces, mem_n):
+    own_members, rows, lanes = pieces[0].shape
     return pl.pallas_call(
-        functools.partial(exchange_out_kernel, mem_n),
-        out_shape=jax.ShapeDtypeStruct((tiles * mem_n, all_rows // mem_n, lanes), jnp.float32),
-        in_specs=[pl.BlockSpec(memory_space=pl.ANY)],
+        functools.partial(join_kernel, mem_n),
+        out_shape=jax.ShapeDtypeStruct((own_members, rows * len(pieces), lanes), jnp.float32),
+        in_specs=[pl.BlockSpec(memory_space=pl.ANY)] * len(pieces),
         out_specs=pl.BlockSpec(memory_space=pl.ANY),
-        scratch_shapes=[
-            pltpu.SemaphoreType.DMA((mem_n,)),
-            pltpu.SemaphoreType.DMA((mem_n,)),
-            pltpu.SemaphoreType.DMA,
-        ],
-        compiler_params=pltpu.CompilerParams(collective_id=1, has_side_effects=True),
-        name="exchange_out",
-    )(tile)
-
-
-def update_kernel(members, shared, near, first_row, tile, anom, weight, obs_row, obs_lon, out, current, spread):
-    groups = tile.shape[0] // (BLOCKS * GROUP)
+        scratch_shapes=[pltpu.SemaphoreType.DMA((len(pieces),))],
+        name="join",
+    )(*pieces)
+
+
+def update_kernel(mem_n, members, shared, *refs):
+    near, first_row, anom, weight, obs_row, obs_lon = refs[:6]
+    pieces, results = refs[6 : 6 + mem_n], refs[6 + mem_n : 6 + 2 * mem_n]
+    tile, current, spread, sems = refs[6 + 2 * mem_n :]
+    piece_rows = pieces[0].shape[0]
+    stride = tile.shape[0] // members
+    groups = stride // (SLABS * BLOCKS * GROUP)
     span = GROUP * LANES
+    copies = [
+        pltpu.make_async_copy(piece, tile.at[pl.ds(j * piece_rows, piece_rows)], sems.at[j])
+        for j, piece in enumerate(pieces)
+    ]
+    for copy in copies:
+        copy.start()
+    for copy in copies:
+        copy.wait()
     lane = lax.broadcasted_iota(jnp.int32, (1, LANES), 1)
 
     def step(index, carry):
         block = index // groups
         group = lax.rem(index, groups)
-        starts = [(group * GROUP + r) * BLOCKS + block for r in range(GROUP)]
+        starts = [((group * GROUP + r) * BLOCKS + block) * SLABS for r in range(GROUP)]
         for s in range(SLABS):
             for r in range(GROUP):
                 at = s * span + r * LANES
-                current[:, at : at + LANES] = tile[starts[r], pl.ds(s, members, stride=SLABS), :]
+                current[:, at : at + LANES] = tile[
+                    pl.ds(starts[r] + s, members, stride=stride), :
+                ]
         lons = (block * LANES + lane).astype(jnp.float32)
         for b in range(NB):
             for s in range(SLABS):
@@ -267,28 +271,43 @@
         for s in range(SLABS):
             for r in range(GROUP):
                 at = s * span + r * LANES
-                out[starts[r], pl.ds(s, members, stride=SLABS), :] = current[:, at : at + LANES]
+                tile[pl.ds(starts[r] + s, members, stride=stride), :] = current[
+                    :, at : at + LANES
+                ]
         return carry
 
     lax.fori_loop(0, BLOCKS * groups, step, 0)
-
-
-def update(tile, near, first_row, anom, weight, obs_row, obs_lon, shared):
-    members = tile.shape[1] // SLABS
+    copies = [
+        pltpu.make_async_copy(tile.at[pl.ds(j * piece_rows, piece_rows)], result, sems.at[j])
+        for j, result in enumerate(results)
+    ]
+    for copy in copies:
+        copy.start()
+    for copy in copies:
+        copy.wait()
+
+
+def update(pieces, near, first_row, anom, weight, obs_row, obs_lon, members, shared):
+    mem_n = len(pieces)
+    piece_rows = pieces[0].shape[0]
     whole = pl.BlockSpec(memory_space=pltpu.VMEM)
     scalars = pl.BlockSpec(memory_space=pltpu.SMEM)
+    hbm = pl.BlockSpec(memory_space=pl.ANY)
     return pl.pallas_call(
-        functools.partial(update_kernel, members, shared),
-        out_shape=jax.ShapeDtypeStruct(tile.shape, jnp.float32),
-        in_specs=[scalars, scalars, whole, whole, whole, whole, whole],
-        out_specs=whole,
+        functools.partial(update_kernel, mem_n, members, shared),
+        out_shape=[jax.ShapeDtypeStruct(p.shape, jnp.float32) for p in pieces],
+        in_specs=[scalars, scalars, whole, whole, whole, whole] + [hbm] * mem_n,
+        out_specs=[hbm] * mem_n,
         scratch_shapes=[
+            pltpu.VMEM((mem_n * piece_rows, LANES), jnp.float32),
             pltpu.VMEM((members, SLABS * GROUP * LANES), jnp.float32),
             pltpu.VMEM((3 * members, SLABS * GROUP * LANES), jnp.bfloat16),
+            pltpu.SemaphoreType.DMA((mem_n,)),
         ],
-        compiler_params=pltpu.CompilerParams(vmem_limit_bytes=40 * 1024 * 1024),
+        compiler_params=pltpu.CompilerParams(vmem_limit_bytes=24 * 1024 * 1024),
+        cost_estimate=pl.CostEstimate(flops=4 * 10**10, bytes_accessed=10**7, transcendentals=0),
         name="update",
-    )(near, first_row, tile, anom, weight, obs_row, obs_lon)
+    )(near, first_row, anom, weight, obs_row, obs_lon, *pieces)
 
 
 def by_longitude(columns, arrays):
@@ -322,7 +341,23 @@
     part_columns = all_columns // parts
     width = part_columns // mem_n
     tiles = part_columns // LANES
-    prior = prior.reshape(own_members, SLABS, part_columns)
+    tiles = part_columns // LANES
+    prior = prior.reshape(own_members, SLABS, tiles, LANES).transpose(0, 2, 1, 3)
+    prior = prior.reshape(own_members, tiles * SLABS, LANES)
+    piece = tiles * SLABS // (mem_n * HALVES)
+    peers = [jnp.bitwise_xor(m, j) for j in range(mem_n)]
+    pairs = [[(i, i ^ j) for i in range(mem_n)] for j in range(mem_n)]
+
+    def swap(parts):
+        return [parts[0]] + [lax.ppermute(parts[j], "mem", pairs[j]) for j in range(1, mem_n)]
+
+    arrived = []
+    for half in range(HALVES):
+        sent = [
+            lax.dynamic_slice_in_dim(prior, (peer * HALVES + half) * piece, piece, 1)
+            for peer in peers
+        ]
+        arrived.append(swap(sent))
 
     columns, levels, values, variances = by_longitude(
         obs_column, [obs_column, obs_level, obs_value, obs_variance]
@@ -331,16 +366,19 @@
     flat_column = columns.reshape(-1)
     flat_level = levels.reshape(-1)
     slab = (flat_level % own_levels) * parts + flat_column // part_columns
+    part_column = flat_column % part_columns
     owned = flat_level // own_levels == c
-    picked = jnp.take(prior, flat_column % part_columns, axis=2)
-    mine = (slab[None, :] == jnp.arange(SLABS, dtype=jnp.int32)[:, None]) & owned[None, :]
-    picked = jnp.sum(jnp.where(mine[None], picked, 0.0), axis=1)
-    picked = jnp.pad(picked, ((0, -own_members % 8), (0, 0)))
-
-    prior = prior.reshape(own_members, SLABS, tiles, LANES).transpose(2, 0, 1, 3)
-    prior = prior.reshape(tiles, own_members * SLABS, LANES)
-    tile, obs = exchange_in(prior, picked, mem_n, col_n)
-    obs = obs[:, :own_members].reshape(members, NB, P_SIZE)
+    row = part_column // LANES * SLABS + slab
+    picked = pick(
+        prior.reshape(own_members * tiles * SLABS, LANES),
+        jnp.where(owned, row, 0),
+        part_column % LANES,
+        owned.astype(jnp.int32),
+        own_members,
+    )
+    obs = gather(picked, mem_n, col_n)[:, :, :own_members]
+    obs = jnp.take(obs, jnp.stack(peers), axis=0).transpose(0, 2, 1, 3)
+    obs = obs.reshape(members, NB, P_SIZE)
 
     rows = (columns // NLON).astype(jnp.float32)
     lons = (columns % NLON).astype(jnp.float32)
@@ -382,12 +420,24 @@
     obs_lon = jnp.pad(lons, ((0, 0), (0, extra)))[:, :, None]
 
     slabs = jnp.arange(SLABS, dtype=jnp.int32)
-    first_row = ((slabs % parts) * part_columns + m * width) // NLON
-    done = update(
-        tile, near_blocks(columns), first_row, anom, weight, obs_row, obs_lon, parts == 1
-    )
-    out = exchange_out(done, mem_n).reshape(tiles, own_members, SLABS, LANES)
-    out = out.transpose(1, 2, 0, 3)
+    near = near_blocks(columns)
+    pieces = []
+    for half in range(HALVES):
+        first_row = (slabs % parts) * part_columns + m * width + half * (width // HALVES)
+        done = update(
+            [p.reshape(own_members * piece, LANES) for p in arrived[half]],
+            near,
+            first_row // NLON,
+            anom,
+            weight,
+            obs_row,
+            obs_lon,
+            members,
+            parts == 1,
+        )
+        pieces += [p.reshape(own_members, piece, LANES) for p in swap(done)]
+    out = join(pieces, mem_n).reshape(own_members, tiles, SLABS, LANES)
+    out = out.transpose(0, 2, 1, 3)
     return out.reshape(own_members, own_levels, all_columns)
 
 

time: 354 us -> 501 us (1.42)
  Pallas kernels: 262 us -> 411 us
  local copies, waits for them, and re-layouts: 70.2 us -> 17.6 us
  waiting for transfers between devices: 0 us -> 40.2 us
  starting transfers between devices: 0 us -> 16.7 us
    pallas_call x3 -> x5, Pallas kernels: 262 us -> 411 us  [the longest x1 239 us: join(): pl.pallas_call(functools.partial(join_kernel, mem_n), out_shape=jax.Shape...]
    ppermute x0 -> x12, waiting for transfers between devices: none -> 40.2 us  [swap(): lax.ppermute(parts[j], 'mem', pairs[j])]
    unnamed x13 -> x39, local copies, waits for them, and re-layouts: 39.1 us -> 7.08 us
    reshape x3 -> x1, local copies, waits for them, and re-layouts: 17.6 us -> 0.17 us  [local(): obs = obs.reshape(members, NB, P_SIZE)]
    ppermute x0 -> x12, starting transfers between devices: none -> 16.7 us  [swap(): lax.ppermute(parts[j], 'mem', pairs[j])]
    gather x1, local copies, waits for them, and re-layouts: 11.7 us -> 1.57 us  [local(): obs = jnp.take(obs, jnp.stack(peers), axis=0).transpose(0, 2, 1, 3)]
    dynamic_slice x0 -> x1, local copies, waits for them, and re-layouts: none -> 5.96 us  [local(): lax.dynamic_slice_in_dim(prior, (peer * HALVES + half) * piece, piece, 1)]
    reduce_sum x1 -> x0, other arithmetic: 5.87 us -> none  [local(): picked = jnp.sum(jnp.where(mine[None], picked, 0.0), axis=1)]
  transfers between devices with their start and end apart: 0 -> 12, of which waited for: 0 -> 2; matrix products, arithmetic and copies ran while one was open for 0% -> 4% of each run, Pallas kernels for 0% -> 34%
where the time goes in v2:
time: 501 us
  Pallas kernels  411 us (82%)
  waiting for transfers between devices  40.2 us (8%)
  local copies, waits for them, and re-layouts  17.6 us (4%)
  starting transfers between devices  16.7 us (3%)
  other arithmetic  9.28 us (2%)
  matrix products  5.63 us (1%)
    pallas_call x1, Pallas kernels, join(): pl.pallas_call(functools.partial(join_kernel, mem_n), out_shape=jax.Shape...  239 us
    pallas_call x2, Pallas kernels, update(): pl.pallas_call(functools.partial(update_kernel, mem_n, members, shared),...  91.8 us
    pallas_call x1, Pallas kernels, gather(): pl.pallas_call(functools.partial(gather_kernel, mem_n, col_n), out_shape=...  59.6 us
    ppermute x12, waiting for transfers between devices, swap(): lax.ppermute(parts[j], 'mem', pairs[j])  40.2 us
    pallas_call x1, Pallas kernels, pick(): pl.pallas_call(functools.partial(pick_kernel, own_members), out_shape=jax...  20.7 us
    ppermute x12, starting transfers between devices, swap(): lax.ppermute(parts[j], 'mem', pairs[j])  16.7 us
  transfers between devices with their start and end apart: 12, of which 2 were waited for; matrix products, arithmetic and copies ran while one was open for 4% of the time, Pallas kernels for 34%

profile of v2, /device:TPU:0, one launch (start us, length us, event | category | flops | bytes accessed | tf_op | source)
XLA Modules:
  0.0 501.5 jit_solution(8564114089733567574)
XLA Ops:
  0.0 6.0 %constant_dynamic-slice_fusion = (f32[20,96,128]{2,1,0:T(8,128)}, f32[20,96,128]{2,1,0:T(8,128)}, f32[20,96,128]{2,1,0:T(8,128)}, f32[20,96,128]{2,1,0:T(8,128)S...) fusion(f32[20,768,128]{2,1,0:T(8,128)} %bitcast.107, ...), kind=kLoop, calls=%fused_computation.108 | loop fusion | bytes 15728672 | tf_op jit(solution)/shard_map/dynamic_slice | solution.py:357
  6.0 3.9 collective-permute-start.8
  9.9 0.5 collective-permute-start.7
  10.4 0.1 collective-permute-start.6
  10.4 2.9 collective-permute-start.2
  13.4 0.5 collective-permute-start.1
  13.9 0.1 iota_compare_fusion.2
  14.0 0.6 convert_reduce_fusion
  14.6 0.6 select_reduce_fusion.2
  15.3 0.1 fusion.45
  15.4 0.1 fusion.32
  15.5 0.1 reshape.464
  15.6 0.3 reduce_or.9
  15.9 0.1 copy.34
  16.1 0.0 copy-start
  16.1 3.2 copy-done
  19.3 20.7 %pick.1.picked = f32[8,24,128]{2,1,0:T(8,128)S(1)} custom-call(s32[1024]{0:T(1024)S(1)} %get-tuple-element.52.row, s32[1024]{0:T(1024)S(1)} %get-tuple-element.51.lane, s32[1024]{0:T(1024)S(1)} %fusion.47.owned, f32[15360,128]{1,0:T(8,128)S(1)} %bitcast.108), custom_call_target="tpu_custom_call" | custom-call | flops 10000000000 | bytes 10000000 | tf_op jit(solution)/shard_map/pick/pallas_call | solution.py:95
  40.0 0.6 copy-done.3
  40.6 59.6 %gather.8 = f32[4,8,24,128]{3,2,1,0:T(8,128)} custom-call(f32[8,24,128]{2,1,0:T(8,128)} %copy-done.3), custom_call_target="tpu_custom_call" | custom-call | flops 20000000000 | bytes 1000000 | tf_op jit(solution)/shard_map/gather/pallas_call | solution.py:156
  100.2 1.6 gather_fusion
  101.8 0.1 compare_and_fusion
  101.9 0.1 select_bitcast_fusion
  102.0 0.0 copy-start.15
  102.0 0.0 copy-start.16
  102.0 0.1 copy.36
  102.1 0.2 reshape.467
  102.3 0.4 slice_reduce_fusion.1
  102.6 0.1 copy.50
  102.8 0.2 multiply_reduce_fusion.1
  103.0 0.8 copy.51
  103.9 0.2 copy.43.refs_5_
  104.1 0.2 copy.42.refs_4_
  104.4 0.6 select_reduce_fusion.1
  105.0 1.0 multiply_subtract_fusion
  106.0 3.5 convolution_multiply_fusion
  109.5 2.1 fusion.51
  111.6 0.2 multiply_reduce_fusion
  111.9 0.9 subtract_bitcast_fusion
  112.9 0.9 select_maximum_fusion
  113.8 2.1 copy.41
  115.8 1.1 reduce-precision_convert_fusion.1
  117.0 1.2 reduce-precision_convert_fusion
  118.1 0.4 pad_maximum_fusion.refs_3_
  118.5 0.3 fusion.12.refs_2_
  118.8 0.0 collective-permute-done.8
  118.8 1.8 collective-permute-start
  120.6 0.0 collective-permute-done.7
  120.6 0.0 collective-permute-done.6
  120.6 45.9 %update.3 = (f32[1920,128]{1,0:T(8,128)S(1)}, f32[1920,128]{1,0:T(8,128)S(1)}, f32[1920,128]{1,0:T(8,128)S(1)}, f32[1920,128]{1,0:T(8,128)S(1)}) custom-call(s32[2,7,6]{2,1,0:T(8,128)S(1)} %convert_element_type.37.refs_0_, s32[4]{0:T(128)S(1)} %rem.134.refs_1_, bf16[2,560,240]{2,1,0:T(8,128)(2,1)S(1)} %fusion.12.refs_2_, ...), custom_call_target="tpu_custom_call" | custom-call | flops 40000000000 | bytes 10000000 | tf_op jit(solution)/shard_map/update/pallas_call | solution.py:296
  166.5 0.4 collective-permute-start.9
  166.9 1.7 collective-permute-start.10
  168.6 0.0 collective-permute-done.2
  168.6 1.4 collective-permute-start.11
  170.1 45.9 %update.2 = (f32[1920,128]{1,0:T(8,128)S(1)}, f32[1920,128]{1,0:T(8,128)S(1)}, f32[1920,128]{1,0:T(8,128)S(1)}, f32[1920,128]{1,0:T(8,128)S(1)}) custom-call(s32[2,7,6]{2,1,0:T(8,128)S(1)} %convert_element_type.37.refs_0_, s32[4]{0:T(128)S(1)} %add.177.refs_1_, bf16[2,560,240]{2,1,0:T(8,128)(2,1)S(1)} %fusion.12.refs_2_, ...), custom_call_target="tpu_custom_call" | custom-call | flops 40000000000 | bytes 10000000 | tf_op jit(solution)/shard_map/update/pallas_call | solution.py:296
  216.0 0.9 copy-done.2
  216.9 0.3 collective-permute-start.3
  217.3 1.7 collective-permute-start.4
  219.0 1.4 collective-permute-start.5
  220.4 21.2 %collective-permute-done.3 = f32[1920,128]{1,0:T(8,128)S(1)} collective-permute-done((f32[1920,128]{1,0:T(8,128)S(1)}, f32[1920,128]{1,0:T(8,128)S(1)}, u32[]{:S(2)}, u32[]{:S(2)}) %collective-permute-start.3) | collective-permute-done | bytes 983072 | tf_op jit(solution)/shard_map/ppermute | solution.py:352
  241.6 19.0 %collective-permute-done.4 = f32[1920,128]{1,0:T(8,128)S(1)} collective-permute-done((f32[1920,128]{1,0:T(8,128)S(1)}, f32[1920,128]{1,0:T(8,128)S(1)}, u32[]{:S(2)}, u32[]{:S(2)}) %collective-permute-start.4) | collective-permute-done | bytes 983072 | tf_op jit(solution)/shard_map/ppermute | solution.py:352
  260.6 0.0 collective-permute-done.5
  260.7 1.0 copy-done.12
  261.6 0.3 copy-done.11
  261.9 239.4 %join.1 = f32[20,768,128]{2,1,0:T(8,128)} custom-call(f32[20,96,128]{2,1,0:T(8,128)} %bitcast.112, f32[20,96,128]{2,1,0:T(8,128)} %bitcast.118, f32[20,96,128]{2,1,0:T(8,128)} %bitcast.119, f32[20,96,128]{2,1,0:T(8,128)} %bitcast.120, f32[20,96,128]{2,1,0:T(8,128)} %bitcast.111, f32[20,96,128]{2,1,0:T(8,128)} %bitcast.115, f32[20,96,128]{2,1,0:T(8,128)} %bitcast.116, ...), custom_call_target="tpu_custom_call" | custom-call | tf_op jit(solution)/shard_map/join/pallas_call | solution.py:194
  (54 shorter events, 0.3 us)
Async XLA Ops:
  0.0 13.9 %copy-start.13 = (s32[2,512]{1,0:T(2,128)S(1)}, s32[2,512]{1,0:T(2,128)}, u32[]{:S(2)}) copy-start(s32[2,512]{1,0:T(2,128)} %param.6) | copy-start | bytes 12292
  0.0 14.6 %copy-start.14 = (s32[2,512]{1,0:T(2,128)S(1)}, s32[2,512]{1,0:T(2,128)}, u32[]{:S(2)}) copy-start(s32[2,512]{1,0:T(2,128)} %param.7) | copy-start | bytes 12292
  6.0 112.8 %collective-permute-start.8 = (f32[20,96,128]{2,1,0:T(8,128)}, f32[20,96,128]{2,1,0:T(8,128)}, u32[]{:S(2)}, u32[]{:S(2)}) collective-permute-start(f32[20,96,128]{2,1,0:T(8,128)} %get-tuple-element.29), channel_id=1, source_target_pairs={{0,24},{8,16},{16,8},{24,0},{1,25},{9,17},{17,9},{25,1},{2,26},{10... | collective-permute-start | bytes 2949128 | tf_op jit(solution)/shard_map/ppermute | solution.py:352
  9.9 110.7 %collective-permute-start.7 = (f32[20,96,128]{2,1,0:T(8,128)}, f32[20,96,128]{2,1,0:T(8,128)}, u32[]{:S(2)}, u32[]{:S(2)}) collective-permute-start(f32[20,96,128]{2,1,0:T(8,128)} %get-tuple-element.30), channel_id=1, source_target_pairs={{0,16},{8,24},{16,0},{24,8},{1,17},{9,25},{17,1},{25,9},{2,18},{10... | collective-permute-start | bytes 2949128 | tf_op jit(solution)/shard_map/ppermute | solution.py:352
  10.4 110.2 %collective-permute-start.6 = (f32[20,96,128]{2,1,0:T(8,128)}, f32[20,96,128]{2,1,0:T(8,128)}, u32[]{:S(2)}, u32[]{:S(2)}) collective-permute-start(f32[20,96,128]{2,1,0:T(8,128)} %get-tuple-element.31), channel_id=1, source_target_pairs={{0,8},{8,0},{16,24},{24,16},{1,9},{9,1},{17,25},{25,17},{2,10},{10... | collective-permute-start | bytes 2949128 | tf_op jit(solution)/shard_map/ppermute | solution.py:352
  10.4 158.2 %collective-permute-start.2 = (f32[20,96,128]{2,1,0:T(8,128)}, f32[20,96,128]{2,1,0:T(8,128)}, u32[]{:S(2)}, u32[]{:S(2)}) collective-permute-start(f32[20,96,128]{2,1,0:T(8,128)} %get-tuple-element.33), channel_id=1, source_target_pairs={{0,24},{8,16},{16,8},{24,0},{1,25},{9,17},{17,9},{25,1},{2,26},{10... | collective-permute-start | bytes 2949128 | tf_op jit(solution)/shard_map/ppermute | solution.py:352
  13.4 156.7 %collective-permute-start.1 = (f32[20,96,128]{2,1,0:T(8,128)}, f32[20,96,128]{2,1,0:T(8,128)}, u32[]{:S(2)}, u32[]{:S(2)}) collective-permute-start(f32[20,96,128]{2,1,0:T(8,128)} %get-tuple-element.34), channel_id=1, source_target_pairs={{0,16},{8,24},{16,0},{24,8},{1,17},{9,25},{17,1},{25,9},{2,18},{10... | collective-permute-start | bytes 2949128 | tf_op jit(solution)/shard_map/ppermute | solution.py:352
  16.1 3.2 copy-start
  40.0 0.6 copy-start.3
  102.0 2.4 copy-start.15
  102.0 2.4 copy-start.16
  106.0 3.5 copy-start.4
  111.6 4.2 copy-start.5
  115.8 3.0 copy-start.6
  118.8 51.2 %collective-permute-start = (f32[20,96,128]{2,1,0:T(8,128)S(1)}, f32[20,96,128]{2,1,0:T(8,128)S(1)}, u32[]{:S(2)}, u32[]{:S(2)}) collective-permute-start(f32[20,96,128]{2,1,0:T(8,128)S(1)} %copy-done.6), channel_id=1, source_target_pairs={{0,8},{8,0},{16,24},{24,16},{1,9},{9,1},{17,25},{25,17},{2,10},{10... | collective-permute-start | bytes 2949128 | tf_op jit(solution)/shard_map/ppermute | solution.py:352
  166.5 49.5 %copy-start.1 = (f32[1920,128]{1,0:T(8,128)}, f32[1920,128]{1,0:T(8,128)S(1)}, u32[]{:S(2)}) copy-start(f32[1920,128]{1,0:T(8,128)S(1)} %get-tuple-element.17) | copy-start | bytes 2949124
  166.5 52.5 %collective-permute-start.9 = (f32[1920,128]{1,0:T(8,128)S(1)}, f32[1920,128]{1,0:T(8,128)S(1)}, u32[]{:S(2)}, u32[]{:S(2)}) collective-permute-start(f32[1920,128]{1,0:T(8,128)S(1)} %get-tuple-element.18), channel_id=1, source_target_pairs={{0,8},{8,0},{16,24},{24,16},{1,9},{9,1},{17,25},{25,17},{2,10},{10... | collective-permute-start | bytes 2949128 | tf_op jit(solution)/shard_map/ppermute | solution.py:352
  166.9 53.5 %collective-permute-start.10 = (f32[1920,128]{1,0:T(8,128)S(1)}, f32[1920,128]{1,0:T(8,128)S(1)}, u32[]{:S(2)}, u32[]{:S(2)}) collective-permute-start(f32[1920,128]{1,0:T(8,128)S(1)} %get-tuple-element.19), channel_id=1, source_target_pairs={{0,16},{8,24},{16,0},{24,8},{1,17},{9,25},{17,1},{25,9},{2,18},{10... | collective-permute-start | bytes 2949128 | tf_op jit(solution)/shard_map/ppermute | solution.py:352
  168.6 51.8 %collective-permute-start.11 = (f32[1920,128]{1,0:T(8,128)S(1)}, f32[1920,128]{1,0:T(8,128)S(1)}, u32[]{:S(2)}, u32[]{:S(2)}) collective-permute-start(f32[1920,128]{1,0:T(8,128)S(1)} %get-tuple-element.20), channel_id=1, source_target_pairs={{0,24},{8,16},{16,8},{24,0},{1,25},{9,17},{17,9},{25,1},{2,26},{10... | collective-permute-start | bytes 2949128 | tf_op jit(solution)/shard_map/ppermute | solution.py:352
  216.0 1.0 copy-start.2
  216.9 24.7 %collective-permute-start.3 = (f32[1920,128]{1,0:T(8,128)S(1)}, f32[1920,128]{1,0:T(8,128)S(1)}, u32[]{:S(2)}, u32[]{:S(2)}) collective-permute-start(f32[1920,128]{1,0:T(8,128)S(1)} %get-tuple-element.14), channel_id=1, source_target_pairs={{0,8},{8,0},{16,24},{24,16},{1,9},{9,1},{17,25},{25,17},{2,10},{10... | collective-permute-start | bytes 2949128 | tf_op jit(solution)/shard_map/ppermute | solution.py:352
  217.3 43.4 %collective-permute-start.4 = (f32[1920,128]{1,0:T(8,128)S(1)}, f32[1920,128]{1,0:T(8,128)S(1)}, u32[]{:S(2)}, u32[]{:S(2)}) collective-permute-start(f32[1920,128]{1,0:T(8,128)S(1)} %get-tuple-element.15), channel_id=1, source_target_pairs={{0,16},{8,24},{16,0},{24,8},{1,17},{9,25},{17,1},{25,9},{2,18},{10... | collective-permute-start | bytes 2949128 | tf_op jit(solution)/shard_map/ppermute | solution.py:352
  219.0 41.6 %copy-start.7 = (f32[1920,128]{1,0:T(8,128)}, f32[1920,128]{1,0:T(8,128)S(1)}, u32[]{:S(2)}) copy-start(f32[1920,128]{1,0:T(8,128)S(1)} %collective-permute-done.9) | copy-start | bytes 2949124
  219.0 41.6 %collective-permute-start.5 = (f32[1920,128]{1,0:T(8,128)S(1)}, f32[1920,128]{1,0:T(8,128)S(1)}, u32[]{:S(2)}, u32[]{:S(2)}) collective-permute-start(f32[1920,128]{1,0:T(8,128)S(1)} %get-tuple-element.16), channel_id=1, source_target_pairs={{0,24},{8,16},{16,8},{24,0},{1,25},{9,17},{17,9},{25,1},{2,26},{10... | collective-permute-start | bytes 2949128 | tf_op jit(solution)/shard_map/ppermute | solution.py:352
  220.4 40.2 %copy-start.8 = (f32[1920,128]{1,0:T(8,128)}, f32[1920,128]{1,0:T(8,128)S(1)}, u32[]{:S(2)}) copy-start(f32[1920,128]{1,0:T(8,128)S(1)} %collective-permute-done.10) | copy-start | bytes 2949124
  220.4 40.2 %copy-start.9 = (f32[1920,128]{1,0:T(8,128)}, f32[1920,128]{1,0:T(8,128)S(1)}, u32[]{:S(2)}) copy-start(f32[1920,128]{1,0:T(8,128)S(1)} %collective-permute-done.11) | copy-start | bytes 2949124
  241.6 20.0 %copy-start.10 = (f32[1920,128]{1,0:T(8,128)}, f32[1920,128]{1,0:T(8,128)S(1)}, u32[]{:S(2)}) copy-start(f32[1920,128]{1,0:T(8,128)S(1)} %collective-permute-done.3) | copy-start | bytes 2949124
  260.6 1.3 copy-start.11
  260.6 1.0 copy-start.12

commit v3 on v2

--- a/solution.py
+++ b/solution.py
@@ -194,9 +194,10 @@
     return pl.pallas_call(
         functools.partial(join_kernel, mem_n),
         out_shape=jax.ShapeDtypeStruct((own_members, rows * len(pieces), lanes), jnp.float32),
-        in_specs=[pl.BlockSpec(memory_space=pl.ANY)] * len(pieces),
+        in_specs=[pl.BlockSpec(memory_space=pltpu.VMEM)] * len(pieces),
         out_specs=pl.BlockSpec(memory_space=pl.ANY),
         scratch_shapes=[pltpu.SemaphoreType.DMA((len(pieces),))],
+        compiler_params=pltpu.CompilerParams(vmem_limit_bytes=16 * 1024 * 1024),
         name="join",
     )(*pieces)
 
@@ -351,13 +352,15 @@
     def swap(parts):
         return [parts[0]] + [lax.ppermute(parts[j], "mem", pairs[j]) for j in range(1, mem_n)]
 
-    arrived = []
-    for half in range(HALVES):
-        sent = [
-            lax.dynamic_slice_in_dim(prior, (peer * HALVES + half) * piece, piece, 1)
-            for peer in peers
-        ]
-        arrived.append(swap(sent))
+    def fetch(half):
+        return swap(
+            [
+                lax.dynamic_slice_in_dim(prior, (peer * HALVES + half) * piece, piece, 1)
+                for peer in peers
+            ]
+        )
+
+    arrived = [fetch(0)]
 
     columns, levels, values, variances = by_longitude(
         obs_column, [obs_column, obs_level, obs_value, obs_variance]
@@ -376,7 +379,11 @@
         owned.astype(jnp.int32),
         own_members,
     )
-    obs = gather(picked, mem_n, col_n)[:, :, :own_members]
+    obs = gather(picked, mem_n, col_n)
+    for half in range(1, HALVES):
+        prior, arrived[half - 1] = lax.optimization_barrier((prior, arrived[half - 1]))
+        arrived.append(fetch(half))
+    obs = obs[:, :, :own_members]
     obs = jnp.take(obs, jnp.stack(peers), axis=0).transpose(0, 2, 1, 3)
     obs = obs.reshape(members, NB, P_SIZE)
 

time: 501 us -> 228 us (0.46)
  Pallas kernels: 411 us -> 137 us
    pallas_call x1, Pallas kernels: 239 us -> 3.22 us  [join(): pl.pallas_call(functools.partial(join_kernel, mem_n), out_shape=jax.Shape...]
    pallas_call x1, Pallas kernels: 59.6 us -> 24.1 us  [gather(): pl.pallas_call(functools.partial(gather_kernel, mem_n, col_n), out_shape=...]
  transfers between devices with their start and end apart: 12 -> 12, of which waited for: 2 -> 2; matrix products, arithmetic and copies ran while one was open for 4% -> 9% of each run, Pallas kernels for 34% -> 59%
where the time goes in v3:
time: 228 us; the launch traced here: 225 us
  Pallas kernels  137 us (60%)
  waiting for transfers between devices  41.8 us (18%)
  local copies, waits for them, and re-layouts  15.7 us (7%)
  starting transfers between devices  15.1 us (7%)
  other arithmetic  9.17 us (4%)
  matrix products  5.63 us (2%)
    pallas_call x2, Pallas kernels, update(): pl.pallas_call(functools.partial(update_kernel, mem_n, members, shared),...  88.5 us
    ppermute x12, waiting for transfers between devices, swap(): lax.ppermute(parts[j], 'mem', pairs[j])  41.8 us
    pallas_call x1, Pallas kernels, gather(): pl.pallas_call(functools.partial(gather_kernel, mem_n, col_n), out_shape=...  24.1 us
    pallas_call x1, Pallas kernels, pick(): pl.pallas_call(functools.partial(pick_kernel, own_members), out_shape=jax...  20.7 us
    ppermute x12, starting transfers between devices, swap(): lax.ppermute(parts[j], 'mem', pairs[j])  15.1 us
    dynamic_slice x2, local copies, waits for them, and re-layouts, fetch(): lax.dynamic_slice_in_dim(prior, (peer * HALVES + half) * piece, piece, 1)  6.23 us
    unnamed x21, local copies, waits for them, and re-layouts  4.86 us
  transfers between devices with their start and end apart: 12, of which 2 were waited for; matrix products, arithmetic and copies ran while one was open for 9% of the time, Pallas kernels for 59%

profile of v3, /device:TPU:0, one launch (start us, length us, event | category | flops | bytes accessed | tf_op | source)
XLA Modules:
  0.0 224.5 jit_solution(15381334044507574858)
XLA Ops:
  0.0 3.9 %constant_dynamic-slice_fusion.4 = (f32[20,96,128]{2,1,0:T(8,128)}, f32[20,96,128]{2,1,0:T(8,128)}, f32[20,96,128]{2,1,0:T(8,128)}, f32[20,96,128]{2,1,0:T(8,128)S(1)}) fusion(f32[20,768,128]{2,1,0:T(8,128)} %bitcast.107, s32[]{:T(128)S(6)} %select_n.172, s32[]{:T(128)S(6)} %select_n.171, s32[]{:T(128)S(6)} %select_n.170, s32[]{:T(128)S(6)} %select_n.169), kind=kLoop, calls=%fused_computation.112 | loop fusion | bytes 7864336 | tf_op jit(solution)/shard_map/dynamic_slice | solution.py:358
  3.9 3.9 %collective-permute-start.2 = (f32[20,96,128]{2,1,0:T(8,128)}, f32[20,96,128]{2,1,0:T(8,128)S(1)}, u32[]{:S(2)}, u32[]{:S(2)}) collective-permute-start(f32[20,96,128]{2,1,0:T(8,128)} %get-tuple-element.43), channel_id=1, source_target_pairs={{0,24},{8,16},{16,8},{24,0},{1,25},{9,17},{17,9},{25,1},{2,26},{10... | collective-permute-start | bytes 2949128 | tf_op jit(solution)/shard_map/ppermute | solution.py:353
  7.8 0.5 collective-permute-start.1
  8.3 0.1 collective-permute-start
  8.3 0.1 iota_compare_fusion.2
  8.4 0.6 convert_reduce_fusion
  9.0 0.6 select_reduce_fusion.2
  9.7 0.1 fusion.45
  9.9 0.1 fusion.32
  10.0 0.1 reshape.464
  10.1 0.3 reduce_or.9
  10.4 0.1 copy.34
  10.5 0.0 copy-start
  10.6 3.2 %copy-done = f32[20,4,24576]{2,1,0:T(4,128)S(1)} copy-done((f32[20,4,24576]{2,1,0:T(4,128)S(1)}, f32[20,4,24576]{2,1,0:T(4,128)}, u32[]{:S(2)}) %copy-start) | copy-done | bytes 7864344
  13.8 20.7 %pick.1.picked = f32[8,24,128]{2,1,0:T(8,128)S(1)} custom-call(s32[1024]{0:T(1024)S(1)} %get-tuple-element.62.row, s32[1024]{0:T(1024)S(1)} %get-tuple-element.61.lane, s32[1024]{0:T(1024)S(1)} %fusion.47.owned, f32[15360,128]{1,0:T(8,128)S(1)} %bitcast.109), custom_call_target="tpu_custom_call" | custom-call | flops 10000000000 | bytes 10000000 | tf_op jit(solution)/shard_map/pick/pallas_call | solution.py:95
  34.5 0.6 copy-done.1
  35.1 24.1 %gather.8 = f32[4,8,24,128]{3,2,1,0:T(8,128)} custom-call(f32[8,24,128]{2,1,0:T(8,128)} %copy-done.1), custom_call_target="tpu_custom_call" | custom-call | flops 20000000000 | bytes 1000000 | tf_op jit(solution)/shard_map/gather/pallas_call | solution.py:156
  59.2 1.6 gather_fusion
  60.8 0.1 compare_and_fusion
  60.9 0.1 select_bitcast_fusion
  61.0 0.0 copy-start.6
  61.0 0.0 copy-start.7
  61.0 0.1 copy.36
  61.1 0.2 reshape.467
  61.3 0.4 slice_reduce_fusion.1
  61.6 0.1 copy.50
  61.8 0.2 multiply_reduce_fusion.1
  62.0 0.8 copy.51
  62.9 0.2 copy.43.refs_5_
  63.1 0.2 copy.42.refs_4_
  63.4 0.6 select_reduce_fusion.1
  64.0 0.9 multiply_subtract_fusion
  65.0 3.5 %convolution_multiply_fusion = f32[512,512]{1,0:T(8,128)S(1)} fusion(f32[512]{0:T(512)S(1)} %bitcast.143, f32[512]{0:T(512)S(1)} %bitcast.144, f32[512]{0:T(512)S(1)} %bitcast.142, f32[512]{0:T(512)S(1)} %bitcast.141, f32[80,1,512]{0,2,1:T(8,128)} %copy.51, f32[80,1,512]{0,2,1:T(8,128)S(1)} %copy.50, f32[512]{0:T(512)S(1)} %get-tuple-element.78, ...), kind=kOutput, calls=%fused_computation.9 | convolution fusion | flops 261480448 | bytes 1388544 | tf_op jit(solution)/shard_map/kp,kc->pc/dot_general | solution.py:401
  68.5 2.1 fusion.51
  70.6 0.2 multiply_reduce_fusion
  70.9 1.0 subtract_bitcast_fusion
  71.9 0.9 select_maximum_fusion
  72.7 2.1 copy.41
  74.8 1.0 reduce-precision_convert_fusion.1
  75.8 1.2 reduce-precision_convert_fusion
  77.0 0.4 pad_maximum_fusion.refs_3_
  77.4 0.3 fusion.12.refs_2_
  77.7 0.0 collective-permute-done.2
  77.7 0.0 collective-permute-done.1
  77.7 0.0 collective-permute-done
  77.7 2.4 %constant_dynamic-slice_fusion = (f32[20,96,128]{2,1,0:T(8,128)S(1)}, f32[20,96,128]{2,1,0:T(8,128)S(1)}, f32[20,96,128]{2,1,0:T(8,128)S(1)}, f32[20,96,128]{2,1,0:T(8,128)S(1)}) fusion(f32[20,768,128]{2,1,0:T(8,128)} %bitcast.108, s32[]{:T(128)S(6)} %select_n.177, s32[]{:T(128)S(6)} %select_n.176, s32[]{:T(128)S(6)} %select_n.175, s32[]{:T(128)S(6)} %select_n.174), kind=kLoop, calls=%fused_computation.108 | loop fusion | bytes 7864336 | tf_op jit(solution)/shard_map/dynamic_slice | solution.py:358
  80.1 2.1 collective-permute-start.8
  82.2 0.9 collective-permute-start.7
  83.0 0.6 collective-permute-start.6
  83.7 44.4 %update.2 = (f32[1920,128]{1,0:T(8,128)S(1)}, f32[1920,128]{1,0:T(8,128)S(1)}, f32[1920,128]{1,0:T(8,128)S(1)}, f32[1920,128]{1,0:T(8,128)S(1)}) custom-call(s32[2,7,6]{2,1,0:T(8,128)S(1)} %convert_element_type.37.refs_0_, s32[4]{0:T(128)S(1)} %add.177.refs_1_, bf16[2,560,240]{2,1,0:T(8,128)(2,1)S(1)} %fusion.12.refs_2_, ...), custom_call_target="tpu_custom_call" | custom-call | flops 40000000000 | bytes 10000000 | tf_op jit(solution)/shard_map/update/pallas_call | solution.py:297
  128.1 1.5 collective-permute-start.3
  129.6 1.2 collective-permute-start.4
  130.7 0.0 collective-permute-done.8
  130.7 0.9 collective-permute-start.5
  131.7 0.0 collective-permute-done.7
  131.7 44.1 %update.3 = (f32[1920,128]{1,0:T(8,128)S(1)}, f32[1920,128]{1,0:T(8,128)S(1)}, f32[1920,128]{1,0:T(8,128)S(1)}, f32[1920,128]{1,0:T(8,128)S(1)}) custom-call(s32[2,7,6]{2,1,0:T(8,128)S(1)} %convert_element_type.37.refs_0_, s32[4]{0:T(128)S(1)} %rem.134.refs_1_, bf16[2,560,240]{2,1,0:T(8,128)(2,1)S(1)} %fusion.12.refs_2_, ...), custom_call_target="tpu_custom_call" | custom-call | flops 40000000000 | bytes 10000000 | tf_op jit(solution)/shard_map/update/pallas_call | solution.py:297
  175.8 1.5 collective-permute-start.9
  177.2 1.2 collective-permute-start.10
  178.4 0.0 collective-permute-done.3
  178.4 0.9 collective-permute-start.11
  179.3 21.2 %collective-permute-done.9 = f32[1920,128]{1,0:T(8,128)S(1)} collective-permute-done((f32[1920,128]{1,0:T(8,128)S(1)}, f32[1920,128]{1,0:T(8,128)S(1)}, u32[]{:S(2)}, u32[]{:S(2)}) %collective-permute-start.9) | collective-permute-done | bytes 983072 | tf_op jit(solution)/shard_map/ppermute | solution.py:353
  200.5 20.6 %collective-permute-done.10 = f32[1920,128]{1,0:T(8,128)S(1)} collective-permute-done((f32[1920,128]{1,0:T(8,128)S(1)}, f32[1920,128]{1,0:T(8,128)S(1)}, u32[]{:S(2)}, u32[]{:S(2)}) %collective-permute-start.10) | collective-permute-done | bytes 983072 | tf_op jit(solution)/shard_map/ppermute | solution.py:353
  221.1 0.0 collective-permute-done.11
  221.1 3.2 %join.1 = f32[20,768,128]{2,1,0:T(8,128)} custom-call(f32[20,96,128]{2,1,0:T(8,128)S(1)} %bitcast.112, f32[20,96,128]{2,1,0:T(8,128)S(1)} %bitcast.113, f32[20,96,128]{2,1,0:T(8,128)S(1)} %bitcast.114, f32[20,96,128]{2,1,0:T(8,128)S(1)} %bitcast.115, f32[20,96,128]{2,1,0:T(8,128)S(1)} %bitcast.116, f32[20,96,128]{2,1,0:T(8,128)S(1)} %bitcast.117, ...), custom_call_target="tpu_custom_call" | custom-call | tf_op jit(solution)/shard_map/join/pallas_call | solution.py:194
  (37 shorter events, 0.2 us)
Async XLA Ops:
  0.0 8.4 %copy-start.4 = (s32[2,512]{1,0:T(2,128)S(1)}, s32[2,512]{1,0:T(2,128)}, u32[]{:S(2)}) copy-start(s32[2,512]{1,0:T(2,128)} %param.6) | copy-start | bytes 12292
  0.0 9.0 %copy-start.5 = (s32[2,512]{1,0:T(2,128)S(1)}, s32[2,512]{1,0:T(2,128)}, u32[]{:S(2)}) copy-start(s32[2,512]{1,0:T(2,128)} %param.7) | copy-start | bytes 12292
  3.9 73.8 %collective-permute-start.2 = (f32[20,96,128]{2,1,0:T(8,128)}, f32[20,96,128]{2,1,0:T(8,128)S(1)}, u32[]{:S(2)}, u32[]{:S(2)}) collective-permute-start(f32[20,96,128]{2,1,0:T(8,128)} %get-tuple-element.43), channel_id=1, source_target_pairs={{0,24},{8,16},{16,8},{24,0},{1,25},{9,17},{17,9},{25,1},{2,26},{10... | collective-permute-start | bytes 2949128 | tf_op jit(solution)/shard_map/ppermute | solution.py:353
  7.8 69.9 %collective-permute-start.1 = (f32[20,96,128]{2,1,0:T(8,128)}, f32[20,96,128]{2,1,0:T(8,128)}, u32[]{:S(2)}, u32[]{:S(2)}) collective-permute-start(f32[20,96,128]{2,1,0:T(8,128)} %get-tuple-element.44), channel_id=1, source_target_pairs={{0,16},{8,24},{16,0},{24,8},{1,17},{9,25},{17,1},{25,9},{2,18},{10... | collective-permute-start | bytes 2949128 | tf_op jit(solution)/shard_map/ppermute | solution.py:353
  8.3 69.5 %collective-permute-start = (f32[20,96,128]{2,1,0:T(8,128)}, f32[20,96,128]{2,1,0:T(8,128)}, u32[]{:S(2)}, u32[]{:S(2)}) collective-permute-start(f32[20,96,128]{2,1,0:T(8,128)} %get-tuple-element.45), channel_id=1, source_target_pairs={{0,8},{8,0},{16,24},{24,16},{1,9},{9,1},{17,25},{25,17},{2,10},{10... | collective-permute-start | bytes 2949128 | tf_op jit(solution)/shard_map/ppermute | solution.py:353
  10.5 3.2 %copy-start = (f32[20,4,24576]{2,1,0:T(4,128)S(1)}, f32[20,4,24576]{2,1,0:T(4,128)}, u32[]{:S(2)}) copy-start(f32[20,4,24576]{2,1,0:T(4,128)} %param.5) | copy-start | bytes 23592964
  34.5 0.6 copy-start.1
  61.0 2.4 %copy-start.6 = (f32[2,512]{1,0:T(2,128)S(1)}, f32[2,512]{1,0:T(2,128)}, u32[]{:S(2)}) copy-start(f32[2,512]{1,0:T(2,128)} %param.8) | copy-start | bytes 12292
  61.0 2.4 %copy-start.7 = (f32[2,512]{1,0:T(2,128)S(1)}, f32[2,512]{1,0:T(2,128)}, u32[]{:S(2)}) copy-start(f32[2,512]{1,0:T(2,128)} %param.9) | copy-start | bytes 12292
  65.0 3.5 %copy-start.2 = (f32[80,1,512]{0,2,1:T(8,128)S(1)}, f32[80,1,512]{0,2,1:T(8,128)}, u32[]{:S(2)}) copy-start(f32[80,1,512]{0,2,1:T(8,128)} %copy.51) | copy-start | bytes 491524
  70.6 4.2 %copy-start.3 = (f32[1,80,512]{1,2,0:T(8,128)S(1)}, f32[1,80,512]{1,2,0:T(8,128)}, u32[]{:S(2)}) copy-start(f32[1,80,512]{1,2,0:T(8,128)} %get-tuple-element.54) | copy-start | bytes 491524
  80.1 50.6 %collective-permute-start.8 = (f32[20,96,128]{2,1,0:T(8,128)S(1)}, f32[20,96,128]{2,1,0:T(8,128)S(1)}, u32[]{:S(2)}, u32[]{:S(2)}) collective-permute-start(f32[20,96,128]{2,1,0:T(8,128)S(1)} %get-tuple-element.39), channel_id=1, source_target_pairs={{0,24},{8,16},{16,8},{24,0},{1,25},{9,17},{17,9},{25,1},{2,26},{10... | collective-permute-start | bytes 2949128 | tf_op jit(solution)/shard_map/ppermute | solution.py:353
  82.2 49.5 %collective-permute-start.7 = (f32[20,96,128]{2,1,0:T(8,128)S(1)}, f32[20,96,128]{2,1,0:T(8,128)S(1)}, u32[]{:S(2)}, u32[]{:S(2)}) collective-permute-start(f32[20,96,128]{2,1,0:T(8,128)S(1)} %get-tuple-element.40), channel_id=1, source_target_pairs={{0,16},{8,24},{16,0},{24,8},{1,17},{9,25},{17,1},{25,9},{2,18},{10... | collective-permute-start | bytes 2949128 | tf_op jit(solution)/shard_map/ppermute | solution.py:353
  83.0 48.6 %collective-permute-start.6 = (f32[20,96,128]{2,1,0:T(8,128)S(1)}, f32[20,96,128]{2,1,0:T(8,128)S(1)}, u32[]{:S(2)}, u32[]{:S(2)}) collective-permute-start(f32[20,96,128]{2,1,0:T(8,128)S(1)} %get-tuple-element.41), channel_id=1, source_target_pairs={{0,8},{8,0},{16,24},{24,16},{1,9},{9,1},{17,25},{25,17},{2,10},{10... | collective-permute-start | bytes 2949128 | tf_op jit(solution)/shard_map/ppermute | solution.py:353
  128.1 50.3 %collective-permute-start.3 = (f32[1920,128]{1,0:T(8,128)S(1)}, f32[1920,128]{1,0:T(8,128)S(1)}, u32[]{:S(2)}, u32[]{:S(2)}) collective-permute-start(f32[1920,128]{1,0:T(8,128)S(1)} %get-tuple-element.23), channel_id=1, source_target_pairs={{0,8},{8,0},{16,24},{24,16},{1,9},{9,1},{17,25},{25,17},{2,10},{10... | collective-permute-start | bytes 2949128 | tf_op jit(solution)/shard_map/ppermute | solution.py:353
  129.6 49.8 %collective-permute-start.4 = (f32[1920,128]{1,0:T(8,128)S(1)}, f32[1920,128]{1,0:T(8,128)S(1)}, u32[]{:S(2)}, u32[]{:S(2)}) collective-permute-start(f32[1920,128]{1,0:T(8,128)S(1)} %get-tuple-element.24), channel_id=1, source_target_pairs={{0,16},{8,24},{16,0},{24,8},{1,17},{9,25},{17,1},{25,9},{2,18},{10... | collective-permute-start | bytes 2949128 | tf_op jit(solution)/shard_map/ppermute | solution.py:353
  130.7 48.6 %collective-permute-start.5 = (f32[1920,128]{1,0:T(8,128)S(1)}, f32[1920,128]{1,0:T(8,128)S(1)}, u32[]{:S(2)}, u32[]{:S(2)}) collective-permute-start(f32[1920,128]{1,0:T(8,128)S(1)} %get-tuple-element.25), channel_id=1, source_target_pairs={{0,24},{8,16},{16,8},{24,0},{1,25},{9,17},{17,9},{25,1},{2,26},{10... | collective-permute-start | bytes 2949128 | tf_op jit(solution)/shard_map/ppermute | solution.py:353
  175.8 24.8 %collective-permute-start.9 = (f32[1920,128]{1,0:T(8,128)S(1)}, f32[1920,128]{1,0:T(8,128)S(1)}, u32[]{:S(2)}, u32[]{:S(2)}) collective-permute-start(f32[1920,128]{1,0:T(8,128)S(1)} %get-tuple-element.28), channel_id=1, source_target_pairs={{0,8},{8,0},{16,24},{24,16},{1,9},{9,1},{17,25},{25,17},{2,10},{10... | collective-permute-start | bytes 2949128 | tf_op jit(solution)/shard_map/ppermute | solution.py:353
  177.2 43.9 %collective-permute-start.10 = (f32[1920,128]{1,0:T(8,128)S(1)}, f32[1920,128]{1,0:T(8,128)S(1)}, u32[]{:S(2)}, u32[]{:S(2)}) collective-permute-start(f32[1920,128]{1,0:T(8,128)S(1)} %get-tuple-element.29), channel_id=1, source_target_pairs={{0,16},{8,24},{16,0},{24,8},{1,17},{9,25},{17,1},{25,9},{2,18},{10... | collective-permute-start | bytes 2949128 | tf_op jit(solution)/shard_map/ppermute | solution.py:353
  178.4 42.7 %collective-permute-start.11 = (f32[1920,128]{1,0:T(8,128)S(1)}, f32[1920,128]{1,0:T(8,128)S(1)}, u32[]{:S(2)}, u32[]{:S(2)}) collective-permute-start(f32[1920,128]{1,0:T(8,128)S(1)} %get-tuple-element.30), channel_id=1, source_target_pairs={{0,24},{8,16},{16,8},{24,0},{1,25},{9,17},{17,9},{25,1},{2,26},{10... | collective-permute-start | bytes 2949128 | tf_op jit(solution)/shard_map/ppermute | solution.py:353
